TPU v7x, 32 devices: a whole 2x2x4 slice. The times are simulated.
32 devices in a mesh: rep: 8 (over y, x, core), tp: 4 (over z).
Axes of the slice: x: 2, y: 2, z: 4, core: 2. Of those that a mesh axis runs over, the one named last changes fastest.
Arguments:
- hidden: bfloat16 [4096, 8192], P('rep'), may hold values from -36 to 36
- segment_ids: int32 [8, 512], P('rep'), may hold values from 0 to 3, never falling along the last dimension, each value on 1 to 256 neighbouring positions
- norm_gain: bfloat16 [8192], replicated, may hold values from 0.5 to 2
- qkv_weight: bfloat16 [8192, 10240], P(('rep', 'tp')), may hold values from -2 to 2
- qkv_bias: bfloat16 [10240], replicated, may hold values from -13 to 13
Outputs:
- attended: bfloat16 [4096, 8192], P('rep', 'tp')
- block_peak: bfloat16 [64, 80], P(None, 'tp')
All inputs are finite; a program needn't handle non-finite values.
Results may differ from a plain program's by a relative error of at most 0.007.
The roundings to bfloat16 on the way count: a program that leaves them out, or rounds other values in their place, can miss the bound.
Values may be sent and summed in bfloat16 or wider, within the bound.
No kernel may reach another device: no remote copies, remote signals or barrier semaphores. Data moves between devices by JAX's collectives and lax.ppermute only.
A program may use at most 512 MiB of HBM per device.

v0:
```python
import math

import jax
import jax.numpy as jnp
from jax import lax
from jax.sharding import PartitionSpec as P

HEADS = 64
KV = 8
HD = 128
BLOCK = 128


theta_base = 1000000.0
code_limit = 448.0


def as_sent(shard):
    return jax.tree.map(lambda a: a.astype(jnp.bfloat16) if a.dtype == jnp.float32 else a, shard)


def partner_2(value, axis, stride):
    mask = 2**stride
    pairs = [(source, source ^ mask) for source in range(lax.axis_size(axis))]
    return lax.ppermute(value, axis, pairs)


def coarse_code(scaled):
    magnitude = jnp.abs(scaled)
    step_size = jnp.full_like(magnitude, 2.0 ** (-9))
    for exponent in range(-5, 9):
        step_size = jnp.where(magnitude >= 2.0**exponent, 2.0 ** (exponent - 3), step_size)
    return jnp.sign(scaled) * jnp.floor(magnitude / step_size + 0.5) * step_size


def tile_peaks(weight, row_block, col_block):
    row_count, col_count = weight.shape
    tile_view = jnp.abs(weight).reshape(
        row_count // row_block, row_block, col_count // col_block, col_block
    )
    return jnp.max(tile_view, axis=(1, 3))


def tile_scales(peak_tiles):
    return (peak_tiles.astype(jnp.float32) + 1e-06) / code_limit


def encode(weight, peak_tiles, row_block, col_block):
    row_count, col_count = weight.shape
    tile_view = weight.astype(jnp.float32).reshape(
        row_count // row_block, row_block, col_count // col_block, col_block
    )
    scaled = tile_view / tile_scales(peak_tiles)[:, None, :, None]
    return coarse_code(scaled).astype(jnp.bfloat16).reshape(row_count, col_count)


def decode(code_tiles, peak_tiles, block_side):
    row_count, col_count = code_tiles.shape
    tile_view = code_tiles.astype(jnp.float32).reshape(
        row_count // block_side, block_side, col_count // block_side, block_side
    )
    scaled = tile_view * tile_scales(peak_tiles)[:, None, :, None]
    return scaled.astype(jnp.bfloat16).reshape(row_count, col_count)


def regroup(stacked, n_outer, n_inner):
    col_count = stacked.shape[1]
    reshaped = stacked.reshape(n_outer, n_inner, -1, col_count)
    return jnp.transpose(reshaped, (1, 0, 2, 3)).reshape(-1, col_count)


def rms_norm(hidden_rows, norm_gain):
    values_f = hidden_rows.astype(jnp.float32)
    inverse = lax.rsqrt(jnp.mean(values_f * values_f, axis=-1, keepdims=True) + 1e-06)
    return (values_f * inverse * norm_gain.astype(jnp.float32)).astype(jnp.bfloat16)


def token_positions(segments):
    token_index = jnp.arange(segments.shape[0], dtype=jnp.int32)
    same_doc = (segments[:, None] == segments[None, :]) & (
        token_index[None, :] < token_index[:, None]
    )
    return jnp.sum(same_doc.astype(jnp.int32), axis=1)


def rotary(head_values, position):
    half_width = head_values.shape[-1] // 2
    freq_index = jnp.arange(half_width, dtype=jnp.float32)
    frequency = jnp.exp(freq_index * (-2.0 / head_values.shape[-1]) * math.log(theta_base))
    angles = position.astype(jnp.float32)[:, None] * frequency[None, :]
    shape_out = (head_values.shape[0],) + (1,) * (head_values.ndim - 2) + (half_width,)
    cosine = jnp.cos(angles).reshape(shape_out)
    sine_part = jnp.sin(angles).reshape(shape_out)
    front_half = head_values[..., :half_width]
    back_half = head_values[..., half_width:]
    return jnp.concatenate(
        [front_half * cosine - back_half * sine_part, back_half * cosine + front_half * sine_part],
        axis=-1,
    )


def split_heads(projected, position):
    per_head = HEADS // KV
    token_total = projected.shape[0]
    groups = projected.shape[1] // ((per_head + 2) * HD)
    grouped = projected.reshape(token_total, groups, per_head + 2, HD)
    query_heads = rotary(grouped[:, :, :per_head, :], position).astype(jnp.bfloat16)
    key_heads = rotary(grouped[:, :, per_head, :], position).astype(jnp.bfloat16)
    value_heads = grouped[:, :, per_head + 1, :].astype(jnp.bfloat16)
    return (query_heads, key_heads, value_heads)


def attend(query_heads, key_heads, value_heads, segments, block_rows):
    token_total = query_heads.shape[0]
    token_index = jnp.arange(token_total, dtype=jnp.int32)
    scale_factor = 1.0 / math.sqrt(query_heads.shape[-1])

    def one_block(first_row):
        row_ids = first_row + jnp.arange(block_rows, dtype=jnp.int32)
        allowed = (segments[:, None] == segments[None, :]) & (
            token_index[None, :] <= row_ids[:, None]
        )
        scores = (
            jnp.einsum("tgqd,sgd->gqts", query_heads, key_heads, preferred_element_type=jnp.float32)
            * scale_factor
        )
        scores = jnp.where(allowed, scores, -1e30)
        row_max = jnp.max(scores, axis=-1, keepdims=True)
        weights_raw = jnp.where(allowed, jnp.exp(scores - row_max), 0.0)
        probabilities = (weights_raw / jnp.sum(weights_raw, axis=-1, keepdims=True)).astype(
            jnp.bfloat16
        )
        mixed_out = jnp.einsum(
            "gqts,sgd->tgqd", probabilities, value_heads, preferred_element_type=jnp.float32
        )
        return mixed_out.astype(jnp.bfloat16)

    starts = jnp.arange(token_total // block_rows, dtype=jnp.int32) * block_rows
    pieces = lax.map(one_block, starts)
    return pieces.reshape(token_total, -1)


def shards(hidden, segment_ids, norm_gain, qkv_weight, qkv_bias):
    n_replica = lax.axis_size("rep")
    n_group = lax.axis_size("tp")
    rows_dev, full_width = qkv_weight.shape
    row_block = min(BLOCK, rows_dev)
    shared = BLOCK // row_block
    peak_tiles = tile_peaks(qkv_weight, row_block, BLOCK)
    for bit_index in range(shared.bit_length() - 1):
        partner = partner_2(as_sent(peak_tiles), "tp", bit_index).astype(peak_tiles.dtype)
        peak_tiles = jnp.maximum(peak_tiles, partner)
    code_tiles = encode(qkv_weight, peak_tiles, row_block, BLOCK)
    codes_all, peaks_all = (
        lax.all_gather(code_tiles, "rep", axis=0, tiled=True),
        lax.all_gather(peak_tiles, "rep", axis=0, tiled=True),
    )
    codes_all, peaks_all = (
        lax.all_to_all(codes_all, "tp", split_axis=1, concat_axis=0, tiled=True),
        lax.all_to_all(peaks_all, "tp", split_axis=1, concat_axis=0, tiled=True),
    )
    codes_all = regroup(codes_all, n_group, n_replica)
    peaks_all = regroup(peaks_all, n_group, n_replica)
    block_peak = peaks_all[::shared]
    restored = decode(codes_all, block_peak, BLOCK)
    local_cols = full_width // n_group
    bias_local = lax.dynamic_slice_in_dim(
        qkv_bias, lax.axis_index("tp") * local_cols, local_cols, 0
    )
    segments = segment_ids[0]
    normed = rms_norm(hidden, norm_gain)
    projected = jnp.dot(normed, restored, preferred_element_type=jnp.float32) + bias_local.astype(
        jnp.float32
    )
    query_heads, key_heads, value_heads = split_heads(projected, token_positions(segments))
    attended = attend(query_heads, key_heads, value_heads, segments, min(512, hidden.shape[0]))
    return (attended, block_peak)


def solution(mesh):
    placed = (P("rep", None), P("rep", None), P(), P(("rep", "tp"), None), P())
    return jax.shard_map(
        shards,
        mesh=mesh,
        in_specs=placed,
        out_specs=(P("rep", "tp"), P(None, "tp")),
        check_vma=False,
    )
```

profile of v0, /device:TPU:0, one launch (start us, length us, event | category | flops | bytes accessed | tf_op | source)
XLA Modules:
  0.0 1489.8 jit_solution(14263865552279927291)
XLA Ops:
  7.2 5.2 abs_bitcast_fusion
  12.4 7.9 copy.70
  20.4 3.7 copy.93
  24.1 0.8 bitcast_reduce_fusion
  25.0 3.5 div.49
  28.6 16.5 %multiply_convert_fusion = bf16[256,10240]{0,1:T(8,128)(2,1)} fusion(f32[1280,8,2,128]{3,2,1,0:T(2,128)S(1)} %bitcast.79, bf16[256,10240]{0,1:T(8,128)(2,1)S(1)} %bitcast.81), kind=kLoop, calls=%fused_computation.16 | loop fusion | flops 99614720 | bytes 20971520 | tf_op jit(solution)/shard_map/convert_element_type | solution.py:54
  45.0 10.2 all-gather
  55.4 10.2 all_to_all.29
  65.7 187.7 %all-gather.3.cloned.1.call-done = bf16[2048,10240]{0,1:T(8,128)(2,1)} async-done(((bf16[256,10240]{0,1:T(8,128)(2,1)}), bf16[2048,10240]{0,1:T(8,128)(2,1)}) %all-gather.3.cloned.1.call-update) | async-done | bytes 41943056 | tf_op jit(solution)/shard_map/all_gather | solution.py:155
  253.3 11.5 all-to-all-start
  265.7 1.4 dynamic-slice_convert_fusion
  267.1 5.1 fusion.2
  272.7 0.9 compare_and_fusion.1
  273.6 1.8 multiply_cosine_fusion
  275.6 26.5 %mul.157 = f32[64,128,20,128]{1,0,3,2:T(8,128)} broadcast(f32[64,20]{0,1:T(8,128)S(1)} %add_multiply_fusion), dimensions={0,2} | broadcast | bytes 83891200 | tf_op jit(solution)/shard_map/mul | solution.py:62
  302.2 87.1 %copy.105 = f32[320,8,64,128]{3,1,2,0:T(8,128)} copy(f32[320,8,64,128]{3,2,1,0:T(8,128)} %bitcast.37) | data formatting | bytes 167772160
  389.2 82.4 %copy.77 = f32[8192,2560]{1,0:T(8,128)} copy(f32[8192,2560]{0,1:T(8,128)} %bitcast.75) | data formatting | bytes 167772160 | tf_op jit(solution)/shard_map/mul | solution.py:62
  471.6 695.9 %all-to-all-done = bf16[2048,4,2560]{0,2,1:T(8,128)(2,1)} async-done(((bf16[2048,4,2560]{0,2,1:T(8,128)(2,1)}), bf16[2048,4,2560]{0,2,1:T(8,128)(2,1)}, u32[]{:S(2)}, u32[]{:S(2)}) %all-to-all-start) | async-done | bytes 41943072 | tf_op jit(solution)/shard_map/all_to_all | solution.py:159
  1167.5 41.0 %convert_bitcast_fusion = f32[4,2048,2560]{1,2,0:T(8,128)} fusion(bf16[2048,4,2560]{0,2,1:T(8,128)(2,1)} %all-to-all-done), kind=kLoop, calls=%fused_computation.4 | loop fusion | flops 20971520 | bytes 125829120 | tf_op jit(solution)/shard_map/convert_element_type | solution.py:59
  1208.5 76.7 %copy.72 = f32[4,2048,2560]{2,1,0:T(8,128)} copy(f32[4,2048,2560]{1,2,0:T(8,128)} %convert_bitcast_fusion) | data formatting | bytes 167772160 | tf_op jit(solution)/shard_map/convert_element_type | solution.py:59
  1285.2 55.6 %copy.73 = f32[8,4,256,2560]{3,2,1,0:T(8,128)} copy(f32[8,4,256,2560]{3,2,0,1:T(8,128)} %bitcast.3) | data formatting | bytes 167772160 | tf_op jit(solution)/shard_map/convert_element_type | solution.py:59
  1340.9 66.1 %fusion.1 = bf16[8192,2560]{1,0:T(8,128)(2,1)} fusion(f32[8192,2560]{1,0:T(8,128)} %copy.77, f32[8,4,256,2560]{3,2,1,0:T(8,128)} %copy.73), kind=kLoop, calls=%fused_computation.3 | loop fusion | flops 41943040 | bytes 209715200 | tf_op jit(solution)/shard_map/convert_element_type | solution.py:63
  1407.0 29.8 %fusion.16 = f32[512,2560]{1,0:T(8,128)} fusion(bf16[8192,2560]{1,0:T(8,128)(2,1)} %fusion.1, bf16[512,8192]{1,0:T(8,128)(2,1)} %param.5, f32[8192]{0:T(1024)S(1)} %copy-done.4, f32[512]{0:T(512)S(1)} %copy-done.8, f32[2560]{0:T(1024)S(1)} %copy-done.7), kind=kOutput, calls=%fused_computation.34 | convolution fusion | flops 21492924416 | bytes 55619584 | tf_op jit(solution)/shard_map/dot_general | solution.py:172
  1436.8 5.9 copy.78
  1442.7 4.2 fusion.29
  1447.0 1.1 slice.29
  1448.1 3.8 copy.90
  1451.9 2.7 copy.91
  1455.1 6.0 subtract_convert_fusion
  1461.0 12.3 fusion.30
  1473.3 7.3 fusion.19
  1480.6 2.4 copy.84
  (41 shorter events, 2.4 us)
Async XLA Ops:
  7.2 246.2 %all-gather.3.cloned.1.call-start = ((), (), s32[]{:S(2)}) async-start(), calls=%async_computation.2 | async-start | bytes 47185920 | tf_op jit(solution)/shard_map/all_gather | solution.py:155
  24.1 4.5 slice-start
  25.0 3.5 slice-start.1
  253.3 11.5 copy-start.6
  253.3 12.1 copy-start.3
  253.3 914.2 %all-to-all-start = ((bf16[2048,4,2560]{0,2,1:T(8,128)(2,1)}), bf16[2048,4,2560]{0,2,1:T(8,128)(2,1)}, u32[]{:S(2)}, u32[]{:S(2)}) async-start(bf16[2048,4,2560]{0,2,1:T(8,128)(2,1)} %bitcast.78), calls=%async_computation | async-start | bytes 83886080 | tf_op jit(solution)/shard_map/all_to_all | solution.py:159
  275.6 26.5 %copy-start.5 = (bf16[64,20]{0,1:T(8,128)(2,1)}, bf16[64,20]{0,1:T(8,128)(2,1)S(1)}, u32[]{:S(2)}) copy-start(bf16[64,20]{0,1:T(8,128)(2,1)S(1)} %copy.76) | copy-start | bytes 7684
  1340.9 66.1 %copy-start.4 = (f32[8192]{0:T(1024)S(1)}, f32[8192]{0:T(1024)}, u32[]{:S(2)}) copy-start(f32[8192]{0:T(1024)} %convert_element_type.83) | copy-start | bytes 98308
  1340.9 66.1 %copy-start.7 = (f32[2560]{0:T(1024)S(1)}, f32[2560]{0:T(1024)}, u32[]{:S(2)}) copy-start(f32[2560]{0:T(1024)} %dynamic-slice_convert_fusion) | copy-start | bytes 30724
  1340.9 66.1 %copy-start.8 = (f32[512]{0:T(512)S(1)}, f32[512]{0:T(512)}, u32[]{:S(2)}) copy-start(f32[512]{0:T(512)} %add_rsqrt_fusion) | copy-start | bytes 6148
  1442.7 12.0 copy-start
  1442.7 12.1 copy-start.1
  1451.9 9.2 copy-start.2
Sparse Core Ops, SparseCore 0:
  45.2 208.1 all-gather.2
where the time goes:
time: 1490 us
  waiting for transfers between devices  884 us (59%)
  local copies, waits for them, and re-layouts  364 us (24%)
  other arithmetic  146 us (10%)
  matrix products  49.4 us (3%)
  blocking collectives  20.5 us (1%)
    all_to_all x1, waiting for transfers between devices, shards(): lax.all_to_all(codes_all, 'tp', split_axis=1, concat_axis=0, tiled=True)  696 us
    all_gather x1, waiting for transfers between devices, shards(): lax.all_gather(code_tiles, 'rep', axis=0, tiled=True)  188 us
    convert_element_type x2, local copies, waits for them, and re-layouts, decode(): code_tiles.astype(jnp.float32)  132 us
    mul x2, local copies, waits for them, and re-layouts, decode(): scaled = tile_view * tile_scales(peak_tiles)[:, None, :, None]  109 us
    unnamed x31, local copies, waits for them, and re-layouts  108 us
    convert_element_type x1, other arithmetic, decode(): return scaled.astype(jnp.bfloat16).reshape(row_count, col_count)  66.1 us
    convert_element_type x1, other arithmetic, decode(): code_tiles.astype(jnp.float32)  41 us
    dot_general x1, matrix products, shards(): jnp.dot(normed, restored, preferred_element_type=jnp.float32)  29.8 us
  transfers between devices with their start and end apart: 2, of which 2 were waited for; matrix products, arithmetic and copies ran while one was open for 14% of the time, Pallas kernels for 0%

commit v1 on v0

v1 whole, which is shorter than its diff:
```python
import functools
import math

import jax
import jax.numpy as jnp
import numpy as np
from jax import lax
from jax.experimental import pallas as pl
from jax.experimental.pallas import tpu as pltpu
from jax.sharding import PartitionSpec as P

HEADS = 64
KV = 8
HD = 128
BLOCK = 128
UNIT = 2 * HD
PER_GROUP = (HEADS // KV + 2) * HD // UNIT

theta_base = 1000000.0
code_limit = 448.0
KERNEL_VMEM = 30 * 2**20


def after(value, *others):
    others = tuple(o for o in others if o is not None)
    return lax.optimization_barrier((value,) + others)[0] if others else value


def tile_scale(peak):
    return (peak + 1e-06) / code_limit


def tile_factor(scale):
    return (1.0 / scale) * (1.0 + 1.75e-07)


def restored_tile(tile, scale, factor):
    scaled = tile * factor
    lean = jnp.abs(scaled) * 0.750001
    wide = lean * (2.0**23 + 1.0)
    power = wide - (wide - lean)
    anchor = jnp.maximum(power * (1.5 * 2.0**20), 1.5 * 2.0**14)
    codes = (scaled + anchor) - anchor
    return codes * scale


def restore_kernel(views, table, *refs):
    count = len(refs) // (views + 1)
    sources, targets = refs[: count * views], refs[count * views :]
    tiles = []
    for n, source in enumerate(sources):
        target, shift = targets[n // views], n % views * UNIT
        for row in range(0, source.shape[0], BLOCK):
            for col in range(0, UNIT, BLOCK):
                here = (slice(row, row + BLOCK), slice(col, col + BLOCK))
                there = (here[0], slice(shift + col, shift + col + BLOCK))
                tiles.append((source, here, target, there))
    scales = []
    for source, here, _, _ in tiles:
        peak = jnp.max(jnp.abs(source[here]), axis=0, keepdims=True).astype(jnp.float32)
        scales.append(tile_scale(jnp.max(peak, axis=1, keepdims=True)))
    factors = [tile_factor(scale) for scale in scales]
    for (source, here, target, there), scale, factor in zip(tiles, scales, factors):
        tile = source[here].astype(jnp.float32)
        target[there] = restored_tile(tile, scale, factor).astype(target.dtype)


def restore(weight, table):
    rows = weight.shape[0]
    count, steps = table.shape
    views = 2 if count == 1 and steps % 2 == 0 else 1
    spec_in = [
        pl.BlockSpec(
            (rows, UNIT), functools.partial(lambda o, v, i, tab: (0, tab[o, i * views + v]), o, v)
        )
        for o in range(count)
        for v in range(views)
    ]
    return pl.pallas_call(
        functools.partial(restore_kernel, views),
        grid_spec=pltpu.PrefetchScalarGridSpec(
            num_scalar_prefetch=1,
            grid=(steps // views,),
            in_specs=spec_in,
            out_specs=[pl.BlockSpec((rows, views * UNIT), lambda i, tab: (0, i))] * count,
        ),
        out_shape=[jax.ShapeDtypeStruct((rows, steps * UNIT), weight.dtype)] * count,
        compiler_params=pltpu.CompilerParams(vmem_limit_bytes=KERNEL_VMEM),
        cost_estimate=pl.CostEstimate(
            flops=16 * rows * UNIT * steps * count,
            bytes_accessed=4 * rows * UNIT * steps * count,
            transcendentals=0,
        ),
    )(table, *([weight] * (count * views)))


def peaks_kernel(weight, fence, out):
    lanes = lax.broadcasted_iota(jnp.int32, out.shape, 1)
    sub = lax.broadcasted_iota(jnp.int32, out.shape, 0)

    def step(j, held):
        cols = pl.ds(pl.multiple_of(j * BLOCK, BLOCK), BLOCK)
        for row in range(weight.shape[0] // BLOCK):
            tile = jnp.abs(weight[row * BLOCK : (row + 1) * BLOCK, cols])
            peak = jnp.max(tile, axis=0, keepdims=True).astype(jnp.float32)
            peak = jnp.max(peak, axis=1, keepdims=True)
            held = jnp.where((lanes == j) & (sub == row), peak, held)
        return held

    out[...] = lax.fori_loop(
        0, weight.shape[1] // BLOCK, step, jnp.zeros(out.shape, jnp.float32), unroll=8
    )


def tile_peaks(weight, *others):
    rows, cols = weight.shape
    if rows % BLOCK == 0 and cols // BLOCK <= 128 and rows // BLOCK <= 8:
        held = pl.pallas_call(
            peaks_kernel,
            in_specs=[
                pl.BlockSpec((rows, cols), lambda: (0, 0)),
                pl.BlockSpec(memory_space=pltpu.SMEM),
            ],
            out_shape=jax.ShapeDtypeStruct((8, 128), jnp.float32),
            compiler_params=pltpu.CompilerParams(vmem_limit_bytes=KERNEL_VMEM),
            cost_estimate=pl.CostEstimate(
                flops=2 * rows * cols, bytes_accessed=2 * rows * cols, transcendentals=0
            ),
        )(weight, after(jnp.zeros((1,), jnp.int32), *others))
        return held[: rows // BLOCK, : cols // BLOCK].astype(weight.dtype)
    block = min(BLOCK, rows)
    view = jnp.abs(weight).reshape(rows // block, block, cols // BLOCK, BLOCK)
    return jnp.max(view, axis=(1, 3))


def shared_peaks(weight, shared):
    peaks = tile_peaks(weight)
    for bit in range(shared.bit_length() - 1):
        pairs = [(s, s ^ 2**bit) for s in range(lax.axis_size("tp"))]
        peaks = jnp.maximum(peaks, lax.ppermute(peaks, "tp", pairs))
    return peaks


def restore_plain(weight, peaks):
    rows, cols = weight.shape
    view = weight.astype(jnp.float32).reshape(
        peaks.shape[0], rows // peaks.shape[0], cols // BLOCK, BLOCK
    )
    scale = tile_scale(peaks.astype(jnp.float32)[:, None, :, None])
    held = restored_tile(view, scale, tile_factor(scale))
    return held.astype(weight.dtype).reshape(rows, cols)


def norm_kernel(block, table, hidden, gain, *outs):
    values = hidden[...].astype(jnp.float32)
    mean = jnp.sum(values * values, axis=-1, keepdims=True) * (1.0 / values.shape[1])
    inverse = lax.rsqrt(mean + 1e-06)
    for o, out in enumerate(outs):
        for b in range(out.shape[1] // block):
            cols = pl.ds(pl.multiple_of(table[o, b] * block, block), block)
            part = hidden[:, cols].astype(jnp.float32) * inverse * gain[:, cols]
            out[:, b * block : (b + 1) * block] = part.astype(out.dtype)


def norm(hidden, gain, table, block):
    tokens, depth = hidden.shape
    count, blocks = table.shape
    if block % 128 == 0:
        rows = min(64, tokens)
        return pl.pallas_call(
            functools.partial(norm_kernel, block),
            grid_spec=pltpu.PrefetchScalarGridSpec(
                num_scalar_prefetch=1,
                grid=(tokens // rows,),
                in_specs=[
                    pl.BlockSpec((rows, depth), lambda i, tab: (i, 0)),
                    pl.BlockSpec((1, depth), lambda i, tab: (0, 0)),
                ],
                out_specs=[pl.BlockSpec((rows, blocks * block), lambda i, tab: (i, 0))] * count,
            ),
            out_shape=[jax.ShapeDtypeStruct((tokens, blocks * block), hidden.dtype)] * count,
            compiler_params=pltpu.CompilerParams(vmem_limit_bytes=KERNEL_VMEM),
            cost_estimate=pl.CostEstimate(
                flops=6 * tokens * depth, bytes_accessed=4 * tokens * depth, transcendentals=0
            ),
        )(table, hidden, gain.astype(jnp.float32).reshape(1, depth))
    values = hidden.astype(jnp.float32)
    inverse = lax.rsqrt(jnp.mean(values * values, axis=-1, keepdims=True) + 1e-06)
    normed = (values * inverse * gain.astype(jnp.float32)).astype(hidden.dtype)
    view = normed.reshape(tokens, depth // block, block)
    return [jnp.take(view, table[o], axis=1).reshape(tokens, blocks * block) for o in range(count)]


def product_kernel(offsets, runs, n_x, n_acc, *refs):
    xs, refs = refs[: n_x * runs], refs[n_x * runs :]
    pieces, refs = refs[: len(offsets)], refs[len(offsets) :]
    accs, refs = refs[:n_acc], refs[n_acc:]
    outs, (x_held, w_held, x_sems, w_sems) = refs[:n_x], refs[n_x:]
    height, width = pieces[0].shape[0], outs[0].shape[1]
    group = len(pieces) // runs
    copies = []
    for r in range(runs):
        own = [
            pltpu.make_async_copy(xs[n * runs + r], x_held.at[n, r], x_sems.at[n, r])
            for n in range(n_x)
        ]
        for p in range(r * group, (r + 1) * group):
            own.append(
                pltpu.make_async_copy(
                    pieces[p].at[:, pl.ds(offsets[p], width)],
                    w_held.at[r, pl.ds((p - r * group) * height, height), :],
                    w_sems.at[p],
                )
            )
        copies.append(own)
        for copy in own:
            copy.start()
    for r in range(runs):
        for copy in copies[r]:
            copy.wait()
        for n, out in enumerate(outs):
            part = jnp.dot(x_held[n, r], w_held[r], preferred_element_type=jnp.float32)
            if r > 0:
                part = out[...] + part
            elif n_acc:
                part = accs[n][...] + part
            out[...] = part


def product(xs, pieces, offsets, width, accs=()):
    runs = len(xs[0])
    tokens, depth = xs[0][0].shape
    if pieces[0].shape[0] % 128:
        held = jnp.concatenate([p[:, o : o + width] for p, o in zip(pieces, offsets)], axis=0)
        outs = [
            jnp.dot(jnp.concatenate(x, axis=1), held, preferred_element_type=jnp.float32) for x in xs
        ]
        return [a + o for a, o in zip(accs, outs)] if accs else outs
    count = len(xs)
    return pl.pallas_call(
        functools.partial(product_kernel, tuple(offsets), runs, count, len(accs)),
        in_specs=[pl.BlockSpec(memory_space=pl.ANY)] * (count * runs + len(pieces))
        + [pl.BlockSpec(memory_space=pltpu.VMEM)] * len(accs),
        out_specs=[pl.BlockSpec(memory_space=pltpu.VMEM)] * count,
        out_shape=[jax.ShapeDtypeStruct((tokens, width), jnp.float32)] * count,
        scratch_shapes=[
            pltpu.VMEM((count, runs, tokens, depth), pieces[0].dtype),
            pltpu.VMEM((runs, depth, width), pieces[0].dtype),
            pltpu.SemaphoreType.DMA((count, runs)),
            pltpu.SemaphoreType.DMA((len(pieces),)),
        ],
        compiler_params=pltpu.CompilerParams(vmem_limit_bytes=KERNEL_VMEM),
        cost_estimate=pl.CostEstimate(
            flops=2 * count * tokens * runs * depth * width,
            bytes_accessed=2 * runs * depth * (count * tokens + width) + 4 * count * tokens * width,
            transcendentals=0,
        ),
    )(*[part for x in xs for part in x], *pieces, *accs)


def token_positions(segments):
    index = jnp.arange(segments.shape[0], dtype=jnp.int32)
    same = (segments[:, None] == segments[None, :]) & (index[None, :] < index[:, None])
    return jnp.sum(same.astype(jnp.int32), axis=1)


def rotary_tables(position):
    half = HD // 2
    index = jnp.arange(half, dtype=jnp.float32)
    frequency = jnp.exp(index * (-2.0 / HD) * math.log(theta_base))
    angles = position.astype(jnp.float32)[:, None] * frequency[None, :]
    cosine, sine = jnp.cos(angles), jnp.sin(angles)
    return (
        jnp.concatenate([cosine, cosine], axis=1),
        jnp.concatenate([-sine, sine], axis=1),
    )


def rotate(head, cosine, sine):
    return head * cosine + pltpu.roll(head, HD // 2, 1) * sine


def key_value_kernel(table, own, other, bias, cosine, sine, key, value):
    both = own[...] + other[...] + bias[...]
    key[...] = rotate(both[:, :HD], cosine[...], sine[...]).astype(key.dtype)
    value[...] = both[:, HD:].astype(value.dtype)


def key_value(own, other, bias, cosine, sine, table, dtype):
    tokens = own.shape[0]
    groups = table.shape[0]
    half = pl.BlockSpec((tokens, UNIT), lambda i, tab: (0, i))
    whole = pl.BlockSpec((tokens, HD), lambda i, tab: (0, 0))
    head = pl.BlockSpec((tokens, HD), lambda i, tab: (0, i))
    return pl.pallas_call(
        key_value_kernel,
        grid_spec=pltpu.PrefetchScalarGridSpec(
            num_scalar_prefetch=1,
            grid=(groups,),
            in_specs=[half, half, pl.BlockSpec((1, UNIT), lambda i, tab: (0, tab[i])), whole, whole],
            out_specs=[head, head],
        ),
        out_shape=[jax.ShapeDtypeStruct((tokens, groups * HD), dtype)] * 2,
        compiler_params=pltpu.CompilerParams(vmem_limit_bytes=KERNEL_VMEM),
        cost_estimate=pl.CostEstimate(
            flops=6 * tokens * groups * UNIT, bytes_accessed=10 * tokens * groups * UNIT, transcendentals=0
        ),
    )(table, own, other, bias, cosine, sine)


def attention_kernel(views, table, own, other, *refs):
    biases, (cosine, sine, key, value, seg_rows, seg_cols, _, out) = refs[:views], refs[views:]
    tokens = own.shape[0]
    rows = min(128, tokens)
    scale = math.log2(math.e) / math.sqrt(HD)
    queries = []
    for h in range(own.shape[1] // HD):
        cols = slice(h * HD, (h + 1) * HD)
        bias = biases[h * HD // UNIT][:, h * HD % UNIT : h * HD % UNIT + HD]
        query = own[:, cols] + other[:, cols] + bias
        queries.append(rotate(query, cosine[...], sine[...]).astype(key.dtype))
    count = len(queries)
    for first in range(0, tokens, rows):
        low, high = max(0, first - 256), first + rows
        row = first + lax.broadcasted_iota(jnp.int32, (rows, high - low), 0)
        col = low + lax.broadcasted_iota(jnp.int32, (rows, high - low), 1)
        allowed = (seg_rows[first:high, :] == seg_cols[:, low:high]) & (col <= row)
        scores = lax.dot_general(
            jnp.concatenate([query[first:high, :] for query in queries], axis=0),
            key[low:high, :],
            (((1,), (1,)), ((), ())),
            preferred_element_type=jnp.float32,
        )
        scores = jnp.where(allowed[None], scores.reshape(count, rows, high - low), -1e30)
        weights = jnp.exp2((scores - jnp.max(scores, axis=-1, keepdims=True)) * scale)
        total = jnp.sum(weights, axis=-1, keepdims=True)
        chances = (weights * (1.0 / total)).astype(value.dtype)
        mixed = jnp.dot(
            chances.reshape(count * rows, high - low),
            value[low:high, :],
            preferred_element_type=jnp.float32,
        ).astype(out.dtype)
        for h in range(count):
            out[first:high, h * HD : (h + 1) * HD] = mixed[h * rows : (h + 1) * rows]


def attention(own, other, bias, cosine, sine, key, value, segments, held, table, skip, base, width):
    tokens = own.shape[0]
    count = table.shape[0]
    per_group = HEADS // KV * HD // UNIT
    views = 2 if count % 2 == skip % 2 == base % 2 == 0 else 1
    half = pl.BlockSpec((tokens, views * UNIT), lambda i, tab: (0, skip // views + i))
    whole = pl.BlockSpec((tokens, HD), lambda i, tab: (0, 0))
    head = pl.BlockSpec((tokens, HD), lambda i, tab: (0, (base + i * views) // per_group))
    in_specs = [
        half,
        half,
        *[
            pl.BlockSpec((1, UNIT), functools.partial(lambda v, i, tab: (0, tab[i * views + v]), v))
            for v in range(views)
        ],
        whole,
        whole,
        head,
        head,
        pl.BlockSpec((tokens, 1), lambda i, tab: (0, 0)),
        pl.BlockSpec((1, tokens), lambda i, tab: (0, 0)),
    ]
    args = [table, own, other, *[bias] * views, cosine, sine, key, value]
    args += [segments[:, None], segments[None, :]]
    aliases = {}
    body = functools.partial(attention_kernel, views)
    if held is None:
        body = lambda *refs: attention_kernel(views, *refs[:-1], None, refs[-1])
    else:
        in_specs.append(pl.BlockSpec(memory_space=pl.ANY))
        args.append(held)
        aliases = {len(args) - 1: 0}
    return pl.pallas_call(
        body,
        grid_spec=pltpu.PrefetchScalarGridSpec(
            num_scalar_prefetch=1,
            grid=(count // views,),
            in_specs=in_specs,
            out_specs=pl.BlockSpec((tokens, views * UNIT), lambda i, tab: (0, base // views + i)),
        ),
        out_shape=jax.ShapeDtypeStruct((tokens, width), key.dtype),
        input_output_aliases=aliases,
        compiler_params=pltpu.CompilerParams(vmem_limit_bytes=KERNEL_VMEM),
        cost_estimate=pl.CostEstimate(
            flops=4 * tokens * tokens * UNIT * count,
            bytes_accessed=8 * tokens * UNIT * count,
            transcendentals=tokens * tokens * 2 * count,
        ),
    )(*args)


def peaks_here(weight, peaks, shared, *others):
    n_rep, n_tp = lax.axis_size("rep"), lax.axis_size("tp")
    rep, tp = lax.axis_index("rep"), lax.axis_index("tp")
    if peaks is None:
        peaks = tile_peaks(weight, *others)
    tiles = peaks.shape[1]
    for name, size, index in (("tp", n_tp, tp), ("rep", n_rep, rep)):
        for bit in range(size.bit_length() - 1):
            pairs = [(d, d ^ 2**bit) for d in range(size)]
            got = lax.ppermute(peaks, name, pairs)
            behind = (index >> bit) % 2 == 1
            first, second = jnp.where(behind, got, peaks), jnp.where(behind, peaks, got)
            peaks = jnp.concatenate([first, second], axis=0)
    return lax.dynamic_slice_in_dim(peaks, tp * (tiles // n_tp), tiles // n_tp, 1)[::shared]


def shards(hidden, segment_ids, norm_gain, qkv_weight, qkv_bias):
    n_rep, n_tp = lax.axis_size("rep"), lax.axis_size("tp")
    rep, tp = lax.axis_index("rep"), lax.axis_index("tp")
    rows, full_width = qkv_weight.shape
    shared = max(1, BLOCK // rows)
    groups = KV // n_tp
    local_units = groups * PER_GROUP
    dtype = qkv_weight.dtype

    bits = [2**b for b in range(1, n_rep.bit_length() - 1)]
    n_pieces = 2 ** len(bits)
    core = rep % 2

    def bit_of(step, of_core):
        return bits[(of_core + step) % len(bits)]

    def gather_step(value, step):
        return lax.ppermute(value, "rep", [(r, r ^ bit_of(step, r % 2)) for r in range(n_rep)])

    def to_core(value):
        return lax.ppermute(value, "rep", [(r, r ^ 1) for r in range(n_rep)])

    def to_server(value, shift):
        return lax.ppermute(value, "tp", [(t, (t + shift) % n_tp) for t in range(n_tp)])

    value_units = [g * PER_GROUP + PER_GROUP - 1 for g in range(groups)]
    query_units = [u for u in range(local_units) if u not in value_units]
    order = np.array(value_units + query_units, np.int32)
    counts = [2 * groups, 2 * groups, groups]
    starts = [0, counts[0], counts[0] + counts[1]]

    if shared == 1 and rows % BLOCK == 0:
        peaks = None

        def restored_units(shifts, first, count, *others):
            units = jnp.asarray(order[first : first + count])
            servers = (tp + jnp.asarray(shifts, jnp.int32)) % n_tp
            table = servers[:, None] * local_units + units[None, :]
            return restore(qkv_weight, after(table, *others))

    else:
        peaks = shared_peaks(qkv_weight, shared)
        plain = restore_plain(qkv_weight, peaks).reshape(rows, n_tp, local_units, UNIT)

        def restored_units(shifts, first, count, *others):
            out = []
            for shift in shifts:
                part = lax.dynamic_index_in_dim(plain, (tp + shift) % n_tp, 1, keepdims=False)
                out.append(part[:, order[first : first + count]].reshape(rows, count * UNIT))
            return out

    far = list(range(1, n_tp))
    n_far = len(far)
    own_a = restored_units([0], 0, counts[0])[0]
    far_units = restored_units(far, 0, counts[0]) if far else []
    step_masks = range(n_pieces)
    relative = np.zeros((2, n_pieces), np.int32)
    for k in range(2):
        for m in step_masks:
            for s in range(len(bits)):
                if m >> s & 1:
                    relative[k, m] ^= bit_of(s, k)
    relative = jnp.asarray(relative)
    shifts = jnp.arange(n_tp, dtype=jnp.int32)

    def depth_blocks(of_rep):
        source = of_rep ^ relative[of_rep % 2]
        server = (tp - shifts) % n_tp
        return (source[None, :] * n_tp + server[:, None]).reshape(-1)

    table = jnp.concatenate(
        [depth_blocks(r).reshape(n_tp, n_pieces) for r in (rep, rep ^ 1)], axis=0
    )
    pieces = []
    served = {}
    fences = {}
    n_units = 2 + 3 * n_far

    def arrived(u):
        return () if u < 0 else tuple(pieces[u][1:-1]) + (tuple(pieces[u - 1][-1:]) if u > 0 else ())

    def near(u):
        return pieces[u][min(1, n_pieces - 1)]

    def serve(u, held):
        fence = (near(u - 4),) if u >= 4 else ()
        served[u] = to_server(after(held, *fence), far[(u - 2) % n_far])

    def gather(held):
        u = len(pieces)
        got = [after(held, *arrived(u - 2), *fences.get(u, ()))]
        for step in range(len(bits)):
            got += [gather_step(g, step) for g in got]
        pieces.append(got)

    gather(own_a)
    for u in range(2, 2 + min(n_far, 3)):
        serve(u, far_units[u - 2])
    own_b = restored_units([0], counts[0], counts[1] + counts[2])[0]
    gather(own_b)
    far_units += restored_units(far, starts[1], counts[1])
    far_units += restored_units(far, starts[2], counts[2])
    parts = norm(hidden, norm_gain, table, rows)
    tokens = [[to_core(p) for p in parts[n_tp:]], parts[:n_tp]]
    segments = segment_ids[0]
    cosine, sine = rotary_tables(token_positions(segments))
    bias = qkv_bias.astype(jnp.float32).reshape(1, full_width)
    held = key = value = None
    base = 0
    for c in range(3):
        width = counts[c] * UNIT
        offset = (starts[c] - starts[min(c, 1)]) * UNIT
        columns = tp * local_units + jnp.asarray(order[starts[c] : starts[c] + counts[c]])
        for n in range(n_far):
            u = len(pieces)
            if u not in served:
                serve(u, far_units[u - 2])
            gather(served[u])
        chunk = [p for got in pieces[2 + c * n_far :] for p in got]
        both = pieces[min(c, 1)] + chunk
        offsets = [offset] * n_pieces + [0] * len(chunk)
        if c < 2:
            theirs, mine = product(tokens, both, offsets, width)
            other = to_core(theirs)
            if c == 0:
                fences[n_units - 3] = (theirs, mine)
        else:
            cut = len(both) - n_pieces
            partial = product([x[:-1] for x in tokens], both[:cut], offsets[:cut], width)
            last = functools.partial(product, pieces=both[cut:], offsets=offsets[cut:], width=width)
            other = to_core(last([tokens[0][-1:]], accs=partial[:1])[0])
            mine = last([tokens[1][-1:]], accs=partial[1:])[0]
        skip = 0
        if c == 0:
            skip = groups
            key, value = key_value(mine, other, bias, cosine, sine, columns[:groups], dtype)
        held = attention(
            mine, other, bias, cosine, sine, key, value, segments, held,
            columns[skip:], skip, base, groups * (HEADS // KV) * HD,
        )
        base += counts[c] - skip
        if c == 0:
            block_peak = peaks_here(qkv_weight, peaks, shared)
            fences[n_units - 1] = (held, block_peak)
    return held, block_peak


def solution(mesh):
    placed = (P("rep", None), P("rep", None), P(), P(("rep", "tp"), None), P())
    return jax.shard_map(
        shards,
        mesh=mesh,
        in_specs=placed,
        out_specs=(P("rep", "tp"), P(None, "tp")),
        check_vma=False,
    )
```

time: 1490 us -> 272 us (0.18)
  waiting for transfers between devices: 884 us -> 76.9 us
  local copies, waits for them, and re-layouts: 364 us -> 46.4 us
  other arithmetic: 146 us -> 2.56 us
  Pallas kernels: 0 us -> 68.9 us
  starting transfers between devices: 11.5 us -> 74.5 us
  matrix products: 49.4 us -> 0 us
  blocking collectives: 20.5 us -> 0 us
    all_to_all x1 -> x0, waiting for transfers between devices: 696 us -> none  [shards(): lax.all_to_all(codes_all, 'tp', split_axis=1, concat_axis=0, tiled=True)]
    all_gather x1 -> x0, waiting for transfers between devices: 188 us -> none  [shards(): lax.all_gather(code_tiles, 'rep', axis=0, tiled=True)]
    convert_element_type x2 -> x0, local copies, waits for them, and re-layouts: 132 us -> none  [decode(): code_tiles.astype(jnp.float32)]
    convert_element_type x6 -> x1, other arithmetic: 126 us -> 0.01 us  [rotary_tables(): angles = position.astype(jnp.float32)[:, None] * frequency[None, :]]
    mul x2 -> x0, local copies, waits for them, and re-layouts: 109 us -> none  [decode(): scaled = tile_view * tile_scales(peak_tiles)[:, None, :, None]]
    ppermute x0 -> x54, waiting for transfers between devices: none -> 76.9 us  [the longest x33 43.6 us: gather_step(): lax.ppermute(value, 'rep', [(r, r ^ bit_of(step, r % 2)) for r in range(n...]
    ppermute x0 -> x54, starting transfers between devices: none -> 74.5 us  [the longest x33 39.8 us: gather_step(): lax.ppermute(value, 'rep', [(r, r ^ bit_of(step, r % 2)) for r in range(n...]
    pallas_call x0 -> x16, Pallas kernels: none -> 68.9 us  [the longest x5 28.7 us: product(): pl.pallas_call(functools.partial(product_kernel, tuple(offsets), runs, co...]
  transfers between devices with their start and end apart: 2 -> 54, of which waited for: 2 -> 18; matrix products, arithmetic and copies ran while one was open for 14% -> 1% of each run, Pallas kernels for 0% -> 23%
where the time goes in v1:
time: 272 us; the launch traced here: 271 us
  waiting for transfers between devices  76.9 us (28%)
  starting transfers between devices  74.5 us (27%)
  Pallas kernels  68.9 us (25%)
  local copies, waits for them, and re-layouts  46.4 us (17%)
    unnamed x161, local copies, waits for them, and re-layouts  46.2 us
    ppermute x33, waiting for transfers between devices, gather_step(): lax.ppermute(value, 'rep', [(r, r ^ bit_of(step, r % 2)) for r in range(n...  43.6 us
    ppermute x33, starting transfers between devices, gather_step(): lax.ppermute(value, 'rep', [(r, r ^ bit_of(step, r % 2)) for r in range(n...  39.8 us
    pallas_call x5, Pallas kernels, product(): pl.pallas_call(functools.partial(product_kernel, tuple(offsets), runs, co...  28.7 us
    ppermute x9, starting transfers between devices, to_server(): lax.ppermute(value, 'tp', [(t, (t + shift) % n_tp) for t in range(n_tp)])  27.9 us
    ppermute x9, waiting for transfers between devices, to_server(): lax.ppermute(value, 'tp', [(t, (t + shift) % n_tp) for t in range(n_tp)])  17.2 us
    pallas_call x3, Pallas kernels, attention(): pl.pallas_call(body, grid_spec=pltpu.PrefetchScalarGridSpec(num_scalar_pr...  17 us
    ppermute x5, waiting for transfers between devices, peaks_here(): got = lax.ppermute(peaks, name, pairs)  16 us
  transfers between devices with their start and end apart: 54, of which 18 were waited for; matrix products, arithmetic and copies ran while one was open for 1% of the time, Pallas kernels for 23%

profile of v1, /device:TPU:0, one launch (start us, length us, event | category | flops | bytes accessed | tf_op | source)
XLA Modules:
  0.0 270.6 jit_solution(12287218825836323643)
XLA Ops:
  1.3 2.5 copy-done
  5.7 3.0 %collective-permute-start.7 = (bf16[256,1536]{1,0:T(8,128)(2,1)S(1)}, bf16[256,1536]{1,0:T(8,128)(2,1)S(1)}, u32[]{:S(2)}, u32[]{:S(2)}) collective-permute-start(bf16[256,1536]{1,0:T(8,128)(2,1)S(1)} %shard_map.199.refs_6_.refs_8_), channel_id=1, source_target_pairs={{0,8},{4,20},{8,0},{12,28},{16,24},{20,4},{24,16},{28,12},{1,9},{5... | collective-permute-start | bytes 2359304 | tf_op jit(solution)/shard_map/ppermute | solution.py:431
  8.8 3.5 %shard_map.197 = (bf16[256,1024]{1,0:T(8,128)(2,1)}, bf16[256,1024]{1,0:T(8,128)(2,1)}, bf16[256,1024]{1,0:T(8,128)(2,1)S(1)}) custom-call(s32[3,4]{1,0:T(4,128)S(1)} %get-tuple-element.109.table, bf16[256,10240]{1,0:T(8,128)(2,1)S(1)} %copy-done, bf16[256,10240]{1,0:T(8,128)(2,1)S(1)} %copy-done, bf16[256,10240]{1,0:T(8,128)(2,1)S(1)} %copy-done), custom_call_target="tpu_custom_call" | custom-call | flops 12582912 | bytes 3145728 | tf_op jit(solution)/shard_map/pallas_call | solution.py:79
  15.4 2.5 copy-done.1
  30.5 3.9 %collective-permute-done.1.refs_9_ = bf16[256,1024]{1,0:T(8,128)(2,1)} collective-permute-done((bf16[256,1024]{1,0:T(8,128)(2,1)S(1)}, bf16[256,1024]{1,0:T(8,128)(2,1)}, u32[]{:S(2)}, u32[]{:S(2)}) %collective-permute-start.1) | collective-permute-done | bytes 524320 | tf_op jit(solution)/shard_map/ppermute | solution.py:431
  37.6 2.8 %collective-permute-start.38 = (bf16[4,80]{1,0:T(4,128)(2,1)S(1)}, bf16[4,80]{1,0:T(4,128)(2,1)S(1)}, u32[]{:S(2)}, u32[]{:S(2)}) collective-permute-start(bf16[4,80]{1,0:T(4,128)(2,1)S(1)} %pad_maximum_fusion.5), channel_id=1, source_target_pairs={{0,2},{1,3},{2,0},{3,1},{4,6},{5,7},{6,4},{7,5},{8,10},{9,11},{10,... | collective-permute-start | bytes 1928 | tf_op jit(solution)/shard_map/ppermute | solution.py:407
  40.4 12.9 %collective-permute-done.38 = bf16[4,80]{1,0:T(4,128)(2,1)S(1)} collective-permute-done((bf16[4,80]{1,0:T(4,128)(2,1)S(1)}, bf16[4,80]{1,0:T(4,128)(2,1)S(1)}, u32[]{:S(2)}, u32[]{:S(2)}) %collective-permute-start.38) | collective-permute-done | bytes 672 | tf_op jit(solution)/shard_map/ppermute | solution.py:407
  54.7 2.5 collective-permute-start.5
  57.2 2.8 %copy-done.2 = bf16[256,10240]{1,0:T(8,128)(2,1)S(1)} copy-done((bf16[256,10240]{1,0:T(8,128)(2,1)S(1)}, bf16[256,10240]{1,0:T(8,128)(2,1)}, u32[]{:S(2)}) %copy-start.2) | copy-done | bytes 5242904
  60.0 3.5 %shard_map.196 = (bf16[256,1024]{1,0:T(8,128)(2,1)}, bf16[256,1024]{1,0:T(8,128)(2,1)}, bf16[256,1024]{1,0:T(8,128)(2,1)S(1)}) custom-call(s32[3,4]{1,0:T(4,128)S(1)} %get-tuple-element.110.table, bf16[256,10240]{1,0:T(8,128)(2,1)S(1)} %copy-done.2, bf16[256,10240]{1,0:T(8,128)(2,1)S(1)} %copy-done.2, bf16[256,10240]{1,0:T(8,128)(2,1)S(1)} %copy-done.2), custom_call_target="tpu_custom_call" | custom-call | flops 12582912 | bytes 3145728 | tf_op jit(solution)/shard_map/pallas_call | solution.py:79
  75.2 6.2 %collective-permute-done.20.refs_12_ = bf16[256,1024]{1,0:T(8,128)(2,1)} collective-permute-done((bf16[256,1024]{1,0:T(8,128)(2,1)}, bf16[256,1024]{1,0:T(8,128)(2,1)}, u32[]{:S(2)}, u32[]{:S(2)}) %collective-permute-start.20) | collective-permute-done | bytes 524320 | tf_op jit(solution)/shard_map/ppermute | solution.py:437
  84.1 2.9 %collective-permute-done.22.refs_15_ = bf16[256,1024]{1,0:T(8,128)(2,1)S(1)} collective-permute-done((bf16[256,1024]{1,0:T(8,128)(2,1)S(1)}, bf16[256,1024]{1,0:T(8,128)(2,1)S(1)}, u32[]{:S(2)}, u32[]{:S(2)}) %collective-permute-start.22) | collective-permute-done | bytes 524320 | tf_op jit(solution)/shard_map/ppermute | solution.py:431
  87.8 3.1 %collective-permute-start.23 = (bf16[256,1024]{1,0:T(8,128)(2,1)}, bf16[256,1024]{1,0:T(8,128)(2,1)}, u32[]{:S(2)}, u32[]{:S(2)}) collective-permute-start(bf16[256,1024]{1,0:T(8,128)(2,1)} %collective-permute-done.20.refs_12_), channel_id=1, source_target_pairs={{0,8},{4,20},{8,0},{12,28},{16,24},{20,4},{24,16},{28,12},{1,9},{5... | collective-permute-start | bytes 1572872 | tf_op jit(solution)/shard_map/ppermute | solution.py:431
  90.8 4.3 %collective-permute-start.32 = (bf16[256,1024]{1,0:T(8,128)(2,1)}, bf16[256,1024]{1,0:T(8,128)(2,1)}, u32[]{:S(2)}, u32[]{:S(2)}) collective-permute-start(bf16[256,1024]{1,0:T(8,128)(2,1)} %copy-done.65), channel_id=1, source_target_pairs={{0,3},{1,0},{2,1},{3,2},{4,7},{5,4},{6,5},{7,6},{8,11},{9,8},{10,9... | collective-permute-start | bytes 1572872 | tf_op jit(solution)/shard_map/ppermute | solution.py:437
  95.2 7.9 %collective-permute-done.4.refs_16_ = bf16[256,1024]{1,0:T(8,128)(2,1)S(1)} collective-permute-done((bf16[256,1024]{1,0:T(8,128)(2,1)}, bf16[256,1024]{1,0:T(8,128)(2,1)S(1)}, u32[]{:S(2)}, u32[]{:S(2)}) %collective-permute-start.4) | collective-permute-done | bytes 524320 | tf_op jit(solution)/shard_map/ppermute | solution.py:437
  105.3 3.4 %copy-done.4 = bf16[512,8192]{1,0:T(8,128)(2,1)S(1)} copy-done((bf16[512,8192]{1,0:T(8,128)(2,1)S(1)}, bf16[512,8192]{1,0:T(8,128)(2,1)}, u32[]{:S(2)}) %copy-start.4) | copy-done | bytes 8388632
  108.6 5.8 %shard_map.194 = (bf16[512,1024]{1,0:T(8,128)(2,1)S(1)}, bf16[512,1024]{1,0:T(8,128)(2,1)S(1)}, bf16[512,1024]{1,0:T(8,128)(2,1)S(1)}, bf16[512,1024]{1,0:T(8,12...) custom-call(s32[8,4]{1,0:T(8,128)S(1)} %pad_add_fusion.table, ...), custom_call_target="tpu_custom_call" | custom-call | flops 25165824 | bytes 16777216 | tf_op jit(solution)/shard_map/pallas_call | solution.py:170
  120.2 2.5 copy-done.3
  126.3 8.2 %collective-permute-done.29.refs_23_ = bf16[256,1024]{1,0:T(8,128)(2,1)S(1)} collective-permute-done((bf16[256,1024]{1,0:T(8,128)(2,1)S(1)}, bf16[256,1024]{1,0:T(8,128)(2,1)S(1)}, u32[]{:S(2)}, u32[]{:S(2)}) %collective-permute-start.29) | collective-permute-done | bytes 524320 | tf_op jit(solution)/shard_map/ppermute | solution.py:431
  138.3 11.6 %collective-permute-start.18 = (bf16[256,512]{1,0:T(8,128)(2,1)S(1)}, bf16[256,512]{1,0:T(8,128)(2,1)}, u32[]{:S(2)}, u32[]{:S(2)}) collective-permute-start(bf16[256,512]{1,0:T(8,128)(2,1)S(1)} %get-tuple-element.57), channel_id=1, source_target_pairs={{0,1},{1,2},{2,3},{3,0},{4,5},{5,6},{6,7},{7,4},{8,9},{9,10},{10,1... | collective-permute-start | bytes 786440 | tf_op jit(solution)/shard_map/ppermute | solution.py:437
  154.9 11.1 %shard_map.200 = (f32[512,1024]{1,0:T(8,128)}, f32[512,1024]{1,0:T(8,128)S(1)}) custom-call(bf16[512,1024]{1,0:T(8,128)(2,1)S(1)} %copy-done.36, bf16[512,1024]{1,0:T(8,128)(2,1)} %collective-permute-done.26.refs_1_, bf16[512,1024]{1,0:T(8,128)(2,1)} %collective-permute-done.27.refs_2_, bf16[512,1024]{1,0:T(8,128)(2,1)S(1)} %copy-done.12, ...), custom_call_target="tpu_custom_call" | custom-call | flops 8589934592 | bytes 20971520 | tf_op jit(solution)/shard_map/pallas_call | solution.py:240
  172.4 3.6 %collective-permute-done.24.refs_15_ = bf16[256,1024]{1,0:T(8,128)(2,1)} collective-permute-done((bf16[256,1024]{1,0:T(8,128)(2,1)}, bf16[256,1024]{1,0:T(8,128)(2,1)}, u32[]{:S(2)}, u32[]{:S(2)}) %collective-permute-start.24) | collective-permute-done | bytes 524320 | tf_op jit(solution)/shard_map/ppermute | solution.py:431
  175.9 3.3 %collective-permute-start.46 = (bf16[256,512]{1,0:T(8,128)(2,1)S(1)}, bf16[256,512]{1,0:T(8,128)(2,1)}, u32[]{:S(2)}, u32[]{:S(2)}) collective-permute-start(bf16[256,512]{1,0:T(8,128)(2,1)S(1)} %get-tuple-element.78), channel_id=1, source_target_pairs={{0,2},{1,3},{2,0},{3,1},{4,6},{5,7},{6,4},{7,5},{8,10},{9,11},{10,... | collective-permute-start | bytes 786440 | tf_op jit(solution)/shard_map/ppermute | solution.py:437
  182.1 7.8 %collective-permute-done.48.refs_19_ = bf16[256,1024]{1,0:T(8,128)(2,1)} collective-permute-done((bf16[256,1024]{1,0:T(8,128)(2,1)}, bf16[256,1024]{1,0:T(8,128)(2,1)}, u32[]{:S(2)}, u32[]{:S(2)}) %collective-permute-start.48) | collective-permute-done | bytes 524320 | tf_op jit(solution)/shard_map/ppermute | solution.py:431
  190.0 5.6 %collective-permute-done.35.refs_23_ = bf16[256,1024]{1,0:T(8,128)(2,1)} collective-permute-done((bf16[256,1024]{1,0:T(8,128)(2,1)}, bf16[256,1024]{1,0:T(8,128)(2,1)}, u32[]{:S(2)}, u32[]{:S(2)}) %collective-permute-start.35) | collective-permute-done | bytes 524320 | tf_op jit(solution)/shard_map/ppermute | solution.py:431
  208.3 10.6 %shard_map.207 = (f32[512,1024]{1,0:T(8,128)}, f32[512,1024]{1,0:T(8,128)S(1)}) custom-call(bf16[512,1024]{1,0:T(8,128)(2,1)S(1)} %copy-done.37, bf16[512,1024]{1,0:T(8,128)(2,1)} %collective-permute-done.26.refs_1_, bf16[512,1024]{1,0:T(8,128)(2,1)} %collective-permute-done.27.refs_2_, bf16[512,1024]{1,0:T(8,128)(2,1)S(1)} %copy-done.13, ...), custom_call_target="tpu_custom_call" | custom-call | flops 8589934592 | bytes 20971520 | tf_op jit(solution)/shard_map/pallas_call | solution.py:240
  224.0 2.7 %collective-permute-start.17 = (bf16[256,512]{1,0:T(8,128)(2,1)}, bf16[256,512]{1,0:T(8,128)(2,1)S(1)}, u32[]{:S(2)}, u32[]{:S(2)}) collective-permute-start(bf16[256,512]{1,0:T(8,128)(2,1)} %get-tuple-element.55), channel_id=1, source_target_pairs={{0,3},{1,0},{2,1},{3,2},{4,7},{5,4},{6,5},{7,6},{8,11},{9,8},{10,9... | collective-permute-start | bytes 786440 | tf_op jit(solution)/shard_map/ppermute | solution.py:437
  231.3 5.1 %shard_map.202.refs_8_ = bf16[512,2048]{1,0:T(8,128)(2,1)} custom-call(s32[2]{0:T(128)S(1)} %get-tuple-element.106.refs_0_, f32[512,1024]{1,0:T(8,128)S(1)} %get-tuple-element.69.own.refs_1_, f32[512,1024]{1,0:T(8,128)} %collective-permute-done.36.other.refs_2_, f32[1,10240]{1,0:T(1,128)S(1)} %bitcast.15, f32[1,10240]{1,0:T(1,128)S(1)} %bitcast.16, ...), custom_call_target="tpu_custom_call" | custom-call | flops 536870912 | bytes 2097152 | tf_op jit(solution)/shard_map/pallas_call | solution.py:379
  240.6 5.2 %collective-permute-done.42.refs_2_ = bf16[256,512]{1,0:T(8,128)(2,1)S(1)} collective-permute-done((bf16[256,512]{1,0:T(8,128)(2,1)S(1)}, bf16[256,512]{1,0:T(8,128)(2,1)S(1)}, u32[]{:S(2)}, u32[]{:S(2)}) %collective-permute-start.42) | collective-permute-done | bytes 262176 | tf_op jit(solution)/shard_map/ppermute | solution.py:431
  246.4 4.2 %shard_map.204 = (f32[512,512]{1,0:T(8,128)S(1)}, f32[512,512]{1,0:T(8,128)S(1)}) custom-call(bf16[512,1024]{1,0:T(8,128)(2,1)S(1)} %copy-done.38, bf16[512,1024]{1,0:T(8,128)(2,1)} %collective-permute-done.26.refs_1_, bf16[512,1024]{1,0:T(8,128)(2,1)} %collective-permute-done.27.refs_2_, bf16[512,1024]{1,0:T(8,128)(2,1)S(1)} %copy-done.26, ...), custom_call_target="tpu_custom_call" | custom-call | flops 3221225472 | bytes 11534336 | tf_op jit(solution)/shard_map/pallas_call | solution.py:240
  258.8 7.1 %shard_map.208.refs_8_ = bf16[512,2048]{1,0:T(8,128)(2,1)} custom-call(s32[4]{0:T(128)S(1)} %broadcast_add_fusion.5.table, f32[512,1024]{1,0:T(8,128)S(1)} %copy-done.6, f32[512,1024]{1,0:T(8,128)} %collective-permute-done.53.other, f32[1,10240]{1,0:T(1,128)S(1)} %bitcast.17, f32[1,10240]{1,0:T(1,128)S(1)} %bitcast.18, ...), custom_call_target="tpu_custom_call", output_to_operand_aliasing={{}: (11, {})} | custom-call | flops 1073741824 | bytes 4194304 | tf_op jit(solution)/shard_map/pallas_call | solution.py:379
  265.9 4.8 %shard_map.209 = bf16[512,2048]{1,0:T(8,128)(2,1)} custom-call(s32[2]{0:T(128)S(1)} %broadcast_add_fusion.7.table, f32[512,512]{1,0:T(8,128)S(1)} %shard_map.205.own, f32[512,512]{1,0:T(8,128)} %collective-permute-done.52.other, f32[1,10240]{1,0:T(1,128)S(1)} %bitcast.19, f32[1,10240]{1,0:T(1,128)S(1)} %bitcast.20, ...), custom_call_target="tpu_custom_call", output_to_operand_aliasing={{}: (11, {})} | custom-call | flops 536870912 | bytes 2097152 | tf_op jit(solution)/shard_map/pallas_call | solution.py:379
  (285 shorter events, 102.6 us)
Async XLA Ops:
  5.7 23.3 %collective-permute-start.7 = (bf16[256,1536]{1,0:T(8,128)(2,1)S(1)}, bf16[256,1536]{1,0:T(8,128)(2,1)S(1)}, u32[]{:S(2)}, u32[]{:S(2)}) collective-permute-start(bf16[256,1536]{1,0:T(8,128)(2,1)S(1)} %shard_map.199.refs_6_.refs_8_), channel_id=1, source_target_pairs={{0,8},{4,20},{8,0},{12,28},{16,24},{20,4},{24,16},{28,12},{1,9},{5... | collective-permute-start | bytes 2359304 | tf_op jit(solution)/shard_map/ppermute | solution.py:431
  12.3 15.5 %collective-permute-start = (bf16[256,1024]{1,0:T(8,128)(2,1)}, bf16[256,1024]{1,0:T(8,128)(2,1)S(1)}, u32[]{:S(2)}, u32[]{:S(2)}) collective-permute-start(bf16[256,1024]{1,0:T(8,128)(2,1)} %get-tuple-element.46), channel_id=1, source_target_pairs={{0,1},{1,2},{2,3},{3,0},{4,5},{5,6},{6,7},{7,4},{8,9},{9,10},{10,1... | collective-permute-start | bytes 1572872 | tf_op jit(solution)/shard_map/ppermute | solution.py:437
  13.9 43.3 %collective-permute-start.12 = (bf16[256,1536]{1,0:T(8,128)(2,1)S(1)}, bf16[256,1536]{1,0:T(8,128)(2,1)S(1)}, u32[]{:S(2)}, u32[]{:S(2)}) collective-permute-start(bf16[256,1536]{1,0:T(8,128)(2,1)S(1)} %shard_map.199.refs_6_.refs_8_), channel_id=1, source_target_pairs={{0,16},{4,12},{8,24},{12,4},{16,0},{20,28},{24,8},{28,20},{1,17},{... | collective-permute-start | bytes 2359304 | tf_op jit(solution)/shard_map/ppermute | solution.py:431
  27.8 26.9 %collective-permute-start.11 = (bf16[256,1024]{1,0:T(8,128)(2,1)}, bf16[256,1024]{1,0:T(8,128)(2,1)}, u32[]{:S(2)}, u32[]{:S(2)}) collective-permute-start(bf16[256,1024]{1,0:T(8,128)(2,1)} %get-tuple-element.52), channel_id=1, source_target_pairs={{0,2},{1,3},{2,0},{3,1},{4,6},{5,7},{6,4},{7,5},{8,10},{9,11},{10,... | collective-permute-start | bytes 1572872 | tf_op jit(solution)/shard_map/ppermute | solution.py:437
  29.0 44.6 %collective-permute-start.8 = (bf16[256,1536]{1,0:T(8,128)(2,1)S(1)}, bf16[256,1536]{1,0:T(8,128)(2,1)S(1)}, u32[]{:S(2)}, u32[]{:S(2)}) collective-permute-start(bf16[256,1536]{1,0:T(8,128)(2,1)S(1)} %collective-permute-done.7.refs_7_.refs_9_), channel_id=1, source_target_pairs={{0,16},{4,12},{8,24},{12,4},{16,0},{20,28},{24,8},{28,20},{1,17},{... | collective-permute-start | bytes 2359304 | tf_op jit(solution)/shard_map/ppermute | solution.py:431
  34.4 29.1 %collective-permute-start.13 = (bf16[256,1024]{1,0:T(8,128)(2,1)}, bf16[256,1024]{1,0:T(8,128)(2,1)S(1)}, u32[]{:S(2)}, u32[]{:S(2)}) collective-permute-start(bf16[256,1024]{1,0:T(8,128)(2,1)} %collective-permute-done.1.refs_9_), channel_id=1, source_target_pairs={{0,16},{4,12},{8,24},{12,4},{16,0},{20,28},{24,8},{28,20},{1,17},{... | collective-permute-start | bytes 1572872 | tf_op jit(solution)/shard_map/ppermute | solution.py:431
  37.6 15.7 %collective-permute-start.38 = (bf16[4,80]{1,0:T(4,128)(2,1)S(1)}, bf16[4,80]{1,0:T(4,128)(2,1)S(1)}, u32[]{:S(2)}, u32[]{:S(2)}) collective-permute-start(bf16[4,80]{1,0:T(4,128)(2,1)S(1)} %pad_maximum_fusion.5), channel_id=1, source_target_pairs={{0,2},{1,3},{2,0},{3,1},{4,6},{5,7},{6,4},{7,5},{8,10},{9,11},{10,... | collective-permute-start | bytes 1928 | tf_op jit(solution)/shard_map/ppermute | solution.py:407
  64.4 17.1 %collective-permute-start.20 = (bf16[256,1024]{1,0:T(8,128)(2,1)}, bf16[256,1024]{1,0:T(8,128)(2,1)}, u32[]{:S(2)}, u32[]{:S(2)}) collective-permute-start(bf16[256,1024]{1,0:T(8,128)(2,1)} %get-tuple-element.59), channel_id=1, source_target_pairs={{0,1},{1,2},{2,3},{3,0},{4,5},{5,6},{6,7},{7,4},{8,9},{9,10},{10,1... | collective-permute-start | bytes 1572872 | tf_op jit(solution)/shard_map/ppermute | solution.py:437
  65.7 17.4 %collective-permute-start.14 = (bf16[256,1024]{1,0:T(8,128)(2,1)}, bf16[256,1024]{1,0:T(8,128)(2,1)}, u32[]{:S(2)}, u32[]{:S(2)}) collective-permute-start(bf16[256,1024]{1,0:T(8,128)(2,1)} %collective-permute-done.11.refs_16_), channel_id=1, source_target_pairs={{0,8},{4,20},{8,0},{12,28},{16,24},{20,4},{24,16},{28,12},{1,9},{5... | collective-permute-start | bytes 1572872 | tf_op jit(solution)/shard_map/ppermute | solution.py:431
  70.7 16.2 %collective-permute-start.22 = (bf16[256,1024]{1,0:T(8,128)(2,1)S(1)}, bf16[256,1024]{1,0:T(8,128)(2,1)S(1)}, u32[]{:S(2)}, u32[]{:S(2)}) collective-permute-start(bf16[256,1024]{1,0:T(8,128)(2,1)S(1)} %collective-permute-done.3.refs_13_), channel_id=1, source_target_pairs={{0,16},{4,12},{8,24},{12,4},{16,0},{20,28},{24,8},{28,20},{1,17},{... | collective-permute-start | bytes 1572872 | tf_op jit(solution)/shard_map/ppermute | solution.py:431
  74.5 28.6 %collective-permute-start.4 = (bf16[256,1024]{1,0:T(8,128)(2,1)}, bf16[256,1024]{1,0:T(8,128)(2,1)S(1)}, u32[]{:S(2)}, u32[]{:S(2)}) collective-permute-start(bf16[256,1024]{1,0:T(8,128)(2,1)} %get-tuple-element.48), channel_id=1, source_target_pairs={{0,2},{1,3},{2,0},{3,1},{4,6},{5,7},{6,4},{7,5},{8,10},{9,11},{10,... | collective-permute-start | bytes 1572872 | tf_op jit(solution)/shard_map/ppermute | solution.py:437
  81.4 22.7 %collective-permute-start.9 = (bf16[256,1024]{1,0:T(8,128)(2,1)}, bf16[256,1024]{1,0:T(8,128)(2,1)S(1)}, u32[]{:S(2)}, u32[]{:S(2)}) collective-permute-start(bf16[256,1024]{1,0:T(8,128)(2,1)} %collective-permute-done.5.refs_20_), channel_id=1, source_target_pairs={{0,8},{4,20},{8,0},{12,28},{16,24},{20,4},{24,16},{28,12},{1,9},{5... | collective-permute-start | bytes 1572872 | tf_op jit(solution)/shard_map/ppermute | solution.py:431
  87.8 31.8 %collective-permute-start.23 = (bf16[256,1024]{1,0:T(8,128)(2,1)}, bf16[256,1024]{1,0:T(8,128)(2,1)}, u32[]{:S(2)}, u32[]{:S(2)}) collective-permute-start(bf16[256,1024]{1,0:T(8,128)(2,1)} %collective-permute-done.20.refs_12_), channel_id=1, source_target_pairs={{0,8},{4,20},{8,0},{12,28},{16,24},{20,4},{24,16},{28,12},{1,9},{5... | collective-permute-start | bytes 1572872 | tf_op jit(solution)/shard_map/ppermute | solution.py:431
  90.8 28.7 %collective-permute-start.32 = (bf16[256,1024]{1,0:T(8,128)(2,1)}, bf16[256,1024]{1,0:T(8,128)(2,1)}, u32[]{:S(2)}, u32[]{:S(2)}) collective-permute-start(bf16[256,1024]{1,0:T(8,128)(2,1)} %copy-done.65), channel_id=1, source_target_pairs={{0,3},{1,0},{2,1},{3,2},{4,7},{5,4},{6,5},{7,6},{8,11},{9,8},{10,9... | collective-permute-start | bytes 1572872 | tf_op jit(solution)/shard_map/ppermute | solution.py:437
  95.2 23.1 %collective-permute-start.15 = (bf16[256,1024]{1,0:T(8,128)(2,1)}, bf16[256,1024]{1,0:T(8,128)(2,1)S(1)}, u32[]{:S(2)}, u32[]{:S(2)}) collective-permute-start(bf16[256,1024]{1,0:T(8,128)(2,1)} %collective-permute-done.14.refs_17_), channel_id=1, source_target_pairs={{0,16},{4,12},{8,24},{12,4},{16,0},{20,28},{24,8},{28,20},{1,17},{... | collective-permute-start | bytes 1572872 | tf_op jit(solution)/shard_map/ppermute | solution.py:431
  104.1 21.1 %collective-permute-start.33 = (bf16[256,1024]{1,0:T(8,128)(2,1)}, bf16[256,1024]{1,0:T(8,128)(2,1)}, u32[]{:S(2)}, u32[]{:S(2)}) collective-permute-start(bf16[256,1024]{1,0:T(8,128)(2,1)} %collective-permute-done.20.refs_12_), channel_id=1, source_target_pairs={{0,16},{4,12},{8,24},{12,4},{16,0},{20,28},{24,8},{28,20},{1,17},{... | collective-permute-start | bytes 1572872 | tf_op jit(solution)/shard_map/ppermute | solution.py:431
  118.3 16.8 %collective-permute-start.25 = (bf16[512,1024]{1,0:T(8,128)(2,1)}, bf16[512,1024]{1,0:T(8,128)(2,1)S(1)}, u32[]{:S(2)}, u32[]{:S(2)}) collective-permute-start(bf16[512,1024]{1,0:T(8,128)(2,1)} %get-tuple-element.61), channel_id=1, source_target_pairs={{0,4},{4,0},{8,12},{12,8},{16,20},{20,16},{24,28},{28,24},{1,5},{5... | collective-permute-start | bytes 3145736 | tf_op jit(solution)/shard_map/ppermute | solution.py:434
  119.1 18.3 %collective-permute-start.26 = (bf16[512,1024]{1,0:T(8,128)(2,1)}, bf16[512,1024]{1,0:T(8,128)(2,1)}, u32[]{:S(2)}, u32[]{:S(2)}) collective-permute-start(bf16[512,1024]{1,0:T(8,128)(2,1)} %get-tuple-element.62), channel_id=1, source_target_pairs={{0,4},{4,0},{8,12},{12,8},{16,20},{20,16},{24,28},{28,24},{1,5},{5... | collective-permute-start | bytes 3145736 | tf_op jit(solution)/shard_map/ppermute | solution.py:434
  119.6 18.8 %collective-permute-start.27 = (bf16[512,1024]{1,0:T(8,128)(2,1)}, bf16[512,1024]{1,0:T(8,128)(2,1)}, u32[]{:S(2)}, u32[]{:S(2)}) collective-permute-start(bf16[512,1024]{1,0:T(8,128)(2,1)} %get-tuple-element.63), channel_id=1, source_target_pairs={{0,4},{4,0},{8,12},{12,8},{16,20},{20,16},{24,28},{28,24},{1,5},{5... | collective-permute-start | bytes 3145736 | tf_op jit(solution)/shard_map/ppermute | solution.py:434
  119.6 30.4 %collective-permute-start.28 = (bf16[512,1024]{1,0:T(8,128)(2,1)}, bf16[512,1024]{1,0:T(8,128)(2,1)S(1)}, u32[]{:S(2)}, u32[]{:S(2)}) collective-permute-start(bf16[512,1024]{1,0:T(8,128)(2,1)} %get-tuple-element.64), channel_id=1, source_target_pairs={{0,4},{4,0},{8,12},{12,8},{16,20},{20,16},{24,28},{28,24},{1,5},{5... | collective-permute-start | bytes 3145736 | tf_op jit(solution)/shard_map/ppermute | solution.py:434
  134.4 31.6 %collective-permute-start.40 = (bf16[16,80]{1,0:T(8,128)(2,1)S(1)}, bf16[16,80]{1,0:T(8,128)(2,1)S(1)}, u32[]{:S(2)}, u32[]{:S(2)}) collective-permute-start(bf16[16,80]{1,0:T(8,128)(2,1)S(1)} %pad_maximum_fusion.3), channel_id=1, source_target_pairs={{0,8},{4,12},{8,0},{12,4},{16,24},{20,28},{24,16},{28,20},{1,9},{5... | collective-permute-start | bytes 7688 | tf_op jit(solution)/shard_map/ppermute | solution.py:407
  136.0 30.7 %collective-permute-start.16 = (bf16[256,1024]{1,0:T(8,128)(2,1)S(1)}, bf16[256,1024]{1,0:T(8,128)(2,1)}, u32[]{:S(2)}, u32[]{:S(2)}) collective-permute-start(bf16[256,1024]{1,0:T(8,128)(2,1)S(1)} %copy-done.51), channel_id=1, source_target_pairs={{0,8},{4,20},{8,0},{12,28},{16,24},{20,4},{24,16},{28,12},{1,9},{5... | collective-permute-start | bytes 1572872 | tf_op jit(solution)/shard_map/ppermute | solution.py:431
  137.4 31.1 %collective-permute-start.19 = (bf16[256,1024]{1,0:T(8,128)(2,1)S(1)}, bf16[256,1024]{1,0:T(8,128)(2,1)S(1)}, u32[]{:S(2)}, u32[]{:S(2)}) collective-permute-start(bf16[256,1024]{1,0:T(8,128)(2,1)S(1)} %copy-done.51), channel_id=1, source_target_pairs={{0,16},{4,12},{8,24},{12,4},{16,0},{20,28},{24,8},{28,20},{1,17},{... | collective-permute-start | bytes 1572872 | tf_op jit(solution)/shard_map/ppermute | solution.py:431
  138.3 28.0 %collective-permute-start.18 = (bf16[256,512]{1,0:T(8,128)(2,1)S(1)}, bf16[256,512]{1,0:T(8,128)(2,1)}, u32[]{:S(2)}, u32[]{:S(2)}) collective-permute-start(bf16[256,512]{1,0:T(8,128)(2,1)S(1)} %get-tuple-element.57), channel_id=1, source_target_pairs={{0,1},{1,2},{2,3},{3,0},{4,5},{5,6},{6,7},{7,4},{8,9},{9,10},{10,1... | collective-permute-start | bytes 786440 | tf_op jit(solution)/shard_map/ppermute | solution.py:437
  150.9 18.7 %collective-permute-start.34 = (bf16[256,1024]{1,0:T(8,128)(2,1)}, bf16[256,1024]{1,0:T(8,128)(2,1)}, u32[]{:S(2)}, u32[]{:S(2)}) collective-permute-start(bf16[256,1024]{1,0:T(8,128)(2,1)} %collective-permute-done.32.refs_20_), channel_id=1, source_target_pairs={{0,8},{4,20},{8,0},{12,28},{16,24},{20,4},{24,16},{28,12},{1,9},{5... | collective-permute-start | bytes 1572872 | tf_op jit(solution)/shard_map/ppermute | solution.py:431
  166.0 61.4 %collective-permute-start.36 = (f32[512,1024]{1,0:T(8,128)}, f32[512,1024]{1,0:T(8,128)}, u32[]{:S(2)}, u32[]{:S(2)}) collective-permute-start(f32[512,1024]{1,0:T(8,128)} %get-tuple-element.68), channel_id=1, source_target_pairs={{0,4},{4,0},{8,12},{12,8},{16,20},{20,16},{24,28},{28,24},{1,5},{5... | collective-permute-start | bytes 6291464 | tf_op jit(solution)/shard_map/ppermute | solution.py:434
  169.3 20.7 %collective-permute-start.48 = (bf16[256,1024]{1,0:T(8,128)(2,1)}, bf16[256,1024]{1,0:T(8,128)(2,1)}, u32[]{:S(2)}, u32[]{:S(2)}) collective-permute-start(bf16[256,1024]{1,0:T(8,128)(2,1)} %collective-permute-done.16.refs_17_), channel_id=1, source_target_pairs={{0,16},{4,12},{8,24},{12,4},{16,0},{20,28},{24,8},{28,20},{1,17},{... | collective-permute-start | bytes 1572872 | tf_op jit(solution)/shard_map/ppermute | solution.py:431
  169.6 26.0 %collective-permute-start.35 = (bf16[256,1024]{1,0:T(8,128)(2,1)}, bf16[256,1024]{1,0:T(8,128)(2,1)}, u32[]{:S(2)}, u32[]{:S(2)}) collective-permute-start(bf16[256,1024]{1,0:T(8,128)(2,1)} %collective-permute-done.34.refs_21_), channel_id=1, source_target_pairs={{0,16},{4,12},{8,24},{12,4},{16,0},{20,28},{24,8},{28,20},{1,17},{... | collective-permute-start | bytes 1572872 | tf_op jit(solution)/shard_map/ppermute | solution.py:431
  175.9 45.1 %collective-permute-start.46 = (bf16[256,512]{1,0:T(8,128)(2,1)S(1)}, bf16[256,512]{1,0:T(8,128)(2,1)}, u32[]{:S(2)}, u32[]{:S(2)}) collective-permute-start(bf16[256,512]{1,0:T(8,128)(2,1)S(1)} %get-tuple-element.78), channel_id=1, source_target_pairs={{0,2},{1,3},{2,0},{3,1},{4,6},{5,7},{6,4},{7,5},{8,10},{9,11},{10,... | collective-permute-start | bytes 786440 | tf_op jit(solution)/shard_map/ppermute | solution.py:437
  181.6 45.2 %collective-permute-start.30 = (bf16[256,512]{1,0:T(8,128)(2,1)}, bf16[256,512]{1,0:T(8,128)(2,1)}, u32[]{:S(2)}, u32[]{:S(2)}) collective-permute-start(bf16[256,512]{1,0:T(8,128)(2,1)} %collective-permute-done.18.refs_10_), channel_id=1, source_target_pairs={{0,8},{4,20},{8,0},{12,28},{16,24},{20,4},{24,16},{28,12},{1,9},{5... | collective-permute-start | bytes 786440 | tf_op jit(solution)/shard_map/ppermute | solution.py:431
  220.3 37.8 %collective-permute-start.53 = (f32[512,1024]{1,0:T(8,128)}, f32[512,1024]{1,0:T(8,128)}, u32[]{:S(2)}, u32[]{:S(2)}) collective-permute-start(f32[512,1024]{1,0:T(8,128)} %get-tuple-element.83), channel_id=1, source_target_pairs={{0,4},{4,0},{8,12},{12,8},{16,20},{20,16},{24,28},{28,24},{1,5},{5... | collective-permute-start | bytes 6291464 | tf_op jit(solution)/shard_map/ppermute | solution.py:434
  221.1 15.4 %collective-permute-start.31 = (bf16[256,512]{1,0:T(8,128)(2,1)}, bf16[256,512]{1,0:T(8,128)(2,1)S(1)}, u32[]{:S(2)}, u32[]{:S(2)}) collective-permute-start(bf16[256,512]{1,0:T(8,128)(2,1)} %collective-permute-done.18.refs_10_), channel_id=1, source_target_pairs={{0,16},{4,12},{8,24},{12,4},{16,0},{20,28},{24,8},{28,20},{1,17},{... | collective-permute-start | bytes 786440 | tf_op jit(solution)/shard_map/ppermute | solution.py:431
  (102 other events, 1160.8 us)

commit v2 on v1

--- a/solution.py
+++ b/solution.py
@@ -18,7 +18,7 @@
 
 theta_base = 1000000.0
 code_limit = 448.0
-KERNEL_VMEM = 30 * 2**20
+KERNEL_VMEM = 50 * 2**20
 
 
 def after(value, *others):
@@ -400,15 +400,18 @@
     rep, tp = lax.axis_index("rep"), lax.axis_index("tp")
     if peaks is None:
         peaks = tile_peaks(weight, *others)
-    tiles = peaks.shape[1]
+    blocks, tiles = peaks.shape
+    bits = []
     for name, size, index in (("tp", n_tp, tp), ("rep", n_rep, rep)):
         for bit in range(size.bit_length() - 1):
             pairs = [(d, d ^ 2**bit) for d in range(size)]
-            got = lax.ppermute(peaks, name, pairs)
-            behind = (index >> bit) % 2 == 1
-            first, second = jnp.where(behind, got, peaks), jnp.where(behind, peaks, got)
-            peaks = jnp.concatenate([first, second], axis=0)
-    return lax.dynamic_slice_in_dim(peaks, tp * (tiles // n_tp), tiles // n_tp, 1)[::shared]
+            peaks = jnp.concatenate([peaks, lax.ppermute(peaks, name, pairs)], axis=0)
+            bits.append((index >> bit) % 2 == 1)
+    here = lax.dynamic_slice_in_dim(peaks, tp * (tiles // n_tp), tiles // n_tp, 1)
+    here = here.reshape((2,) * len(bits) + (blocks, tiles // n_tp))
+    for axis, bit in enumerate(reversed(bits)):
+        here = jnp.where(bit, jnp.flip(here, axis), here)
+    return here.reshape(-1, tiles // n_tp)[::shared]
 
 
 def shards(hidden, segment_ids, norm_gain, qkv_weight, qkv_bias):
@@ -536,7 +539,7 @@
             theirs, mine = product(tokens, both, offsets, width)
             other = to_core(theirs)
             if c == 0:
-                fences[n_units - 3] = (theirs, mine)
+                fences[n_units - 2] = (theirs, mine)
         else:
             cut = len(both) - n_pieces
             partial = product([x[:-1] for x in tokens], both[:cut], offsets[:cut], width)
@@ -554,7 +557,8 @@
         base += counts[c] - skip
         if c == 0:
             block_peak = peaks_here(qkv_weight, peaks, shared)
-            fences[n_units - 1] = (held, block_peak)
+            fences[n_units - 1] = (held,)
+            fences[n_units - 2] = fences.get(n_units - 2, ()) + (block_peak,)
     return held, block_peak
 
 

time: 272 us -> 253 us (0.930)
  local copies, waits for them, and re-layouts: 46.4 us -> 13.2 us
  Pallas kernels: 68.9 us -> 88.5 us
  starting transfers between devices: 74.5 us -> 68.9 us
    unnamed x161 -> x97, local copies, waits for them, and re-layouts: 46.2 us -> 12.8 us
    ppermute x5, waiting for transfers between devices: 16 us -> 4.78 us  [peaks_here(): peaks = jnp.concatenate([peaks, lax.ppermute(peaks, name, pairs)], axis=0)]
    pallas_call x5, Pallas kernels: 28.7 us -> 37.2 us  [product(): pl.pallas_call(functools.partial(product_kernel, tuple(offsets), runs, co...]
    ppermute x9, starting transfers between devices: 27.9 us -> 20.4 us  [to_server(): lax.ppermute(value, 'tp', [(t, (t + shift) % n_tp) for t in range(n_tp)])]
    ppermute x7, starting transfers between devices: 1.27 us -> 8.72 us  [to_core(): return lax.ppermute(value, 'rep', [(r, r ^ 1) for r in range(n_rep)])]
    ppermute x9, waiting for transfers between devices: 17.2 us -> 23.2 us  [to_server(): lax.ppermute(value, 'tp', [(t, (t + shift) % n_tp) for t in range(n_tp)])]
    ppermute x33, starting transfers between devices: 39.8 us -> 34.4 us  [gather_step(): lax.ppermute(value, 'rep', [(r, r ^ bit_of(step, r % 2)) for r in range(n...]
    pallas_call x5, Pallas kernels: 12.8 us -> 18.1 us  [restore(): pl.pallas_call(functools.partial(restore_kernel, views), grid_spec=pltpu....]
  transfers between devices with their start and end apart: 54 -> 54, of which waited for: 18 -> 16; matrix products, arithmetic and copies ran while one was open for 1% -> 1% of each run, Pallas kernels for 23% -> 31%
where the time goes in v2:
time: 253 us; the launch traced here: 252 us
  Pallas kernels  88.5 us (35%)
  waiting for transfers between devices  76.7 us (30%)
  starting transfers between devices  68.9 us (27%)
  local copies, waits for them, and re-layouts  13.2 us (5%)
  other arithmetic  3.19 us (1%)
    ppermute x33, waiting for transfers between devices, gather_step(): lax.ppermute(value, 'rep', [(r, r ^ bit_of(step, r % 2)) for r in range(n...  48.8 us
    pallas_call x5, Pallas kernels, product(): pl.pallas_call(functools.partial(product_kernel, tuple(offsets), runs, co...  37.2 us
    ppermute x33, starting transfers between devices, gather_step(): lax.ppermute(value, 'rep', [(r, r ^ bit_of(step, r % 2)) for r in range(n...  34.4 us
    ppermute x9, waiting for transfers between devices, to_server(): lax.ppermute(value, 'tp', [(t, (t + shift) % n_tp) for t in range(n_tp)])  23.2 us
    ppermute x9, starting transfers between devices, to_server(): lax.ppermute(value, 'tp', [(t, (t + shift) % n_tp) for t in range(n_tp)])  20.4 us
    pallas_call x5, Pallas kernels, restore(): pl.pallas_call(functools.partial(restore_kernel, views), grid_spec=pltpu....  18.1 us
    pallas_call x3, Pallas kernels, attention(): pl.pallas_call(body, grid_spec=pltpu.PrefetchScalarGridSpec(num_scalar_pr...  16.8 us
    unnamed x97, local copies, waits for them, and re-layouts  12.8 us
  transfers between devices with their start and end apart: 54, of which 16 were waited for; matrix products, arithmetic and copies ran while one was open for 1% of the time, Pallas kernels for 31%

profile of v2, /device:TPU:0, one launch (start us, length us, event | category | flops | bytes accessed | tf_op | source)
XLA Modules:
  0.0 251.8 jit_solution(2436872562509566989)
XLA Ops:
  2.0 4.7 %shard_map.197 = (bf16[256,1024]{1,0:T(8,128)(2,1)}, bf16[256,1024]{1,0:T(8,128)(2,1)S(1)}, bf16[256,1024]{1,0:T(8,128)(2,1)S(1)}) custom-call(s32[3,4]{1,0:T(4,128)S(1)} %get-tuple-element.97.table, bf16[256,10240]{1,0:T(8,128)(2,1)} %weight.1, bf16[256,10240]{1,0:T(8,128)(2,1)} %weight.1, bf16[256,10240]{1,0:T(8,128)(2,1)} %weight.1), custom_call_target="tpu_custom_call" | custom-call | flops 12582912 | bytes 3145728 | tf_op jit(solution)/shard_map/pallas_call | solution.py:79
  6.7 3.0 %collective-permute-start = (bf16[256,1024]{1,0:T(8,128)(2,1)}, bf16[256,1024]{1,0:T(8,128)(2,1)S(1)}, u32[]{:S(2)}, u32[]{:S(2)}) collective-permute-start(bf16[256,1024]{1,0:T(8,128)(2,1)} %get-tuple-element.46), channel_id=1, source_target_pairs={{0,1},{1,2},{2,3},{3,0},{4,5},{5,6},{6,7},{7,4},{8,9},{9,10},{10,1... | collective-permute-start | bytes 1572872 | tf_op jit(solution)/shard_map/ppermute | solution.py:440
  9.8 3.3 %shard_map.199.refs_6_.refs_8_ = bf16[256,1536]{1,0:T(8,128)(2,1)S(1)} custom-call(s32[1,6]{1,0:T(1,128)S(1)} %add_bitcast_fusion.table, bf16[256,10240]{1,0:T(8,128)(2,1)} %weight.1, bf16[256,10240]{1,0:T(8,128)(2,1)} %weight.1), custom_call_target="tpu_custom_call" | custom-call | flops 6291456 | bytes 1572864 | tf_op jit(solution)/shard_map/pallas_call | solution.py:79
  14.7 4.8 %shard_map.203 = f32[8,128]{1,0:T(8,128)S(1)} custom-call(bf16[256,10240]{1,0:T(8,128)(2,1)} %weight.1, s32[1]{0:T(128)} %constant.137.clone.fence), custom_call_target="tpu_custom_call" | custom-call | flops 5242880 | bytes 5242880 | tf_op jit(solution)/shard_map/pallas_call | solution.py:118
  23.0 2.7 %collective-permute-start.45 = (bf16[4,80]{1,0:T(4,128)(2,1)S(1)}, bf16[4,80]{1,0:T(4,128)(2,1)S(1)}, u32[]{:S(2)}, u32[]{:S(2)}) collective-permute-start(bf16[4,80]{1,0:T(4,128)(2,1)S(1)} %pad_maximum_fusion.4), channel_id=1, source_target_pairs={{0,2},{1,3},{2,0},{3,1},{4,6},{5,7},{6,4},{7,5},{8,10},{9,11},{10,... | collective-permute-start | bytes 1928 | tf_op jit(solution)/shard_map/ppermute | solution.py:408
  25.7 2.3 shard_map.198.refs_8_
  33.5 9.5 %collective-permute-done.1.refs_9_ = bf16[256,1024]{1,0:T(8,128)(2,1)S(1)} collective-permute-done((bf16[256,1024]{1,0:T(8,128)(2,1)S(1)}, bf16[256,1024]{1,0:T(8,128)(2,1)S(1)}, u32[]{:S(2)}, u32[]{:S(2)}) %collective-permute-start.1) | collective-permute-done | bytes 524320 | tf_op jit(solution)/shard_map/ppermute | solution.py:434
  45.8 3.2 %collective-permute-done.47 = bf16[16,80]{1,0:T(8,128)(2,1)S(1)} collective-permute-done((bf16[16,80]{1,0:T(8,128)(2,1)S(1)}, bf16[16,80]{1,0:T(8,128)(2,1)S(1)}, u32[]{:S(2)}, u32[]{:S(2)}) %collective-permute-start.47) | collective-permute-done | bytes 2592 | tf_op jit(solution)/shard_map/ppermute | solution.py:408
  49.6 7.8 %collective-permute-done.11.refs_16_ = bf16[256,1024]{1,0:T(8,128)(2,1)} collective-permute-done((bf16[256,1024]{1,0:T(8,128)(2,1)S(1)}, bf16[256,1024]{1,0:T(8,128)(2,1)}, u32[]{:S(2)}, u32[]{:S(2)}) %collective-permute-start.11) | collective-permute-done | bytes 524320 | tf_op jit(solution)/shard_map/ppermute | solution.py:440
  60.4 5.1 %shard_map.196 = (bf16[256,1024]{1,0:T(8,128)(2,1)S(1)}, bf16[256,1024]{1,0:T(8,128)(2,1)S(1)}, bf16[256,1024]{1,0:T(8,128)(2,1)}) custom-call(s32[3,4]{1,0:T(4,128)S(1)} %get-tuple-element.98.table, bf16[256,10240]{1,0:T(8,128)(2,1)} %weight.1, bf16[256,10240]{1,0:T(8,128)(2,1)} %weight.1, bf16[256,10240]{1,0:T(8,128)(2,1)} %weight.1), custom_call_target="tpu_custom_call" | custom-call | flops 12582912 | bytes 3145728 | tf_op jit(solution)/shard_map/pallas_call | solution.py:79
  70.9 12.2 %collective-permute-done.20.refs_12_ = bf16[256,1024]{1,0:T(8,128)(2,1)} collective-permute-done((bf16[256,1024]{1,0:T(8,128)(2,1)S(1)}, bf16[256,1024]{1,0:T(8,128)(2,1)}, u32[]{:S(2)}, u32[]{:S(2)}) %collective-permute-start.20) | collective-permute-done | bytes 524320 | tf_op jit(solution)/shard_map/ppermute | solution.py:440
  84.3 6.0 %collective-permute-done.22.refs_15_ = bf16[256,1024]{1,0:T(8,128)(2,1)} collective-permute-done((bf16[256,1024]{1,0:T(8,128)(2,1)}, bf16[256,1024]{1,0:T(8,128)(2,1)}, u32[]{:S(2)}, u32[]{:S(2)}) %collective-permute-start.22) | collective-permute-done | bytes 524320 | tf_op jit(solution)/shard_map/ppermute | solution.py:434
  95.2 3.1 %collective-permute-done.4.refs_16_ = bf16[256,1024]{1,0:T(8,128)(2,1)S(1)} collective-permute-done((bf16[256,1024]{1,0:T(8,128)(2,1)S(1)}, bf16[256,1024]{1,0:T(8,128)(2,1)S(1)}, u32[]{:S(2)}, u32[]{:S(2)}) %collective-permute-start.4) | collective-permute-done | bytes 524320 | tf_op jit(solution)/shard_map/ppermute | solution.py:440
  100.6 9.3 %shard_map.194 = (bf16[512,1024]{1,0:T(8,128)(2,1)S(1)}, bf16[512,1024]{1,0:T(8,128)(2,1)S(1)}, bf16[512,1024]{1,0:T(8,128)(2,1)S(1)}, bf16[512,1024]{1,0:T(8,12...) custom-call(s32[8,4]{1,0:T(8,128)S(1)} %pad_add_fusion.table, ...), custom_call_target="tpu_custom_call" | custom-call | flops 25165824 | bytes 16777216 | tf_op jit(solution)/shard_map/pallas_call | solution.py:170
  111.8 7.1 %collective-permute-done.10.refs_22_ = bf16[256,1024]{1,0:T(8,128)(2,1)S(1)} collective-permute-done((bf16[256,1024]{1,0:T(8,128)(2,1)}, bf16[256,1024]{1,0:T(8,128)(2,1)S(1)}, u32[]{:S(2)}, u32[]{:S(2)}) %collective-permute-start.10) | collective-permute-done | bytes 524320 | tf_op jit(solution)/shard_map/ppermute | solution.py:434
  119.0 7.6 %collective-permute-start.32 = (bf16[512,1024]{1,0:T(8,128)(2,1)}, bf16[512,1024]{1,0:T(8,128)(2,1)}, u32[]{:S(2)}, u32[]{:S(2)}) collective-permute-start(bf16[512,1024]{1,0:T(8,128)(2,1)} %get-tuple-element.65), channel_id=1, source_target_pairs={{0,4},{4,0},{8,12},{12,8},{16,20},{20,16},{24,28},{28,24},{1,5},{5... | collective-permute-start | bytes 3145736 | tf_op jit(solution)/shard_map/ppermute | solution.py:437
  129.2 2.8 %shard_map.195 = (bf16[256,512]{1,0:T(8,128)(2,1)S(1)}, bf16[256,512]{1,0:T(8,128)(2,1)S(1)}, bf16[256,512]{1,0:T(8,128)(2,1)S(1)}) custom-call(s32[3,2]{1,0:T(4,128)S(1)} %broadcast_add_fusion.2.table, bf16[256,10240]{1,0:T(8,128)(2,1)} %weight.1, bf16[256,10240]{1,0:T(8,128)(2,1)} %weight.1, bf16[256,10240]{1,0:T(8,128)(2,1)} %weight.1), custom_call_target="tpu_custom_call" | custom-call | flops 6291456 | bytes 1572864 | tf_op jit(solution)/shard_map/pallas_call | solution.py:79
  133.4 4.5 %collective-permute-done.29.refs_23_ = bf16[256,1024]{1,0:T(8,128)(2,1)} collective-permute-done((bf16[256,1024]{1,0:T(8,128)(2,1)}, bf16[256,1024]{1,0:T(8,128)(2,1)}, u32[]{:S(2)}, u32[]{:S(2)}) %collective-permute-start.29) | collective-permute-done | bytes 524320 | tf_op jit(solution)/shard_map/ppermute | solution.py:434
  140.0 5.2 %collective-permute-start.18 = (bf16[256,512]{1,0:T(8,128)(2,1)}, bf16[256,512]{1,0:T(8,128)(2,1)S(1)}, u32[]{:S(2)}, u32[]{:S(2)}) collective-permute-start(bf16[256,512]{1,0:T(8,128)(2,1)} %copy-done.31), channel_id=1, source_target_pairs={{0,1},{1,2},{2,3},{3,0},{4,5},{5,6},{6,7},{7,4},{8,9},{9,10},{10,1... | collective-permute-start | bytes 786440 | tf_op jit(solution)/shard_map/ppermute | solution.py:440
  152.5 12.4 %shard_map.200 = (f32[512,1024]{1,0:T(8,128)}, f32[512,1024]{1,0:T(8,128)}) custom-call(bf16[512,1024]{1,0:T(8,128)(2,1)} %collective-permute-done.32.refs_0_, bf16[512,1024]{1,0:T(8,128)(2,1)} %collective-permute-done.33.refs_1_, bf16[512,1024]{1,0:T(8,128)(2,1)} %collective-permute-done.34.refs_2_, bf16[512,1024]{1,0:T(8,128)(2,1)} %copy-done.3, ...), custom_call_target="tpu_custom_call" | custom-call | flops 8589934592 | bytes 20971520 | tf_op jit(solution)/shard_map/pallas_call | solution.py:240
  168.7 3.6 %collective-permute-start.41 = (bf16[256,512]{1,0:T(8,128)(2,1)S(1)}, bf16[256,512]{1,0:T(8,128)(2,1)S(1)}, u32[]{:S(2)}, u32[]{:S(2)}) collective-permute-start(bf16[256,512]{1,0:T(8,128)(2,1)S(1)} %copy-done.30), channel_id=1, source_target_pairs={{0,2},{1,3},{2,0},{3,1},{4,6},{5,7},{6,4},{7,5},{8,10},{9,11},{10,... | collective-permute-start | bytes 786440 | tf_op jit(solution)/shard_map/ppermute | solution.py:440
  175.3 7.5 %collective-permute-done.43.refs_19_ = bf16[256,1024]{1,0:T(8,128)(2,1)S(1)} collective-permute-done((bf16[256,1024]{1,0:T(8,128)(2,1)S(1)}, bf16[256,1024]{1,0:T(8,128)(2,1)S(1)}, u32[]{:S(2)}, u32[]{:S(2)}) %collective-permute-start.43) | collective-permute-done | bytes 524320 | tf_op jit(solution)/shard_map/ppermute | solution.py:434
  182.8 5.6 %collective-permute-done.31.refs_23_ = bf16[256,1024]{1,0:T(8,128)(2,1)S(1)} collective-permute-done((bf16[256,1024]{1,0:T(8,128)(2,1)S(1)}, bf16[256,1024]{1,0:T(8,128)(2,1)S(1)}, u32[]{:S(2)}, u32[]{:S(2)}) %collective-permute-start.31) | collective-permute-done | bytes 524320 | tf_op jit(solution)/shard_map/ppermute | solution.py:434
  189.2 13.0 %shard_map.207 = (f32[512,1024]{1,0:T(8,128)}, f32[512,1024]{1,0:T(8,128)}) custom-call(bf16[512,1024]{1,0:T(8,128)(2,1)} %collective-permute-done.32.refs_0_, bf16[512,1024]{1,0:T(8,128)(2,1)} %collective-permute-done.33.refs_1_, bf16[512,1024]{1,0:T(8,128)(2,1)} %collective-permute-done.34.refs_2_, bf16[512,1024]{1,0:T(8,128)(2,1)} %copy-done.3, ...), custom_call_target="tpu_custom_call" | custom-call | flops 8589934592 | bytes 20971520 | tf_op jit(solution)/shard_map/pallas_call | solution.py:240
  203.9 2.6 %collective-permute-start.17 = (bf16[256,512]{1,0:T(8,128)(2,1)S(1)}, bf16[256,512]{1,0:T(8,128)(2,1)S(1)}, u32[]{:S(2)}, u32[]{:S(2)}) collective-permute-start(bf16[256,512]{1,0:T(8,128)(2,1)S(1)} %copy-done.28), channel_id=1, source_target_pairs={{0,3},{1,0},{2,1},{3,2},{4,7},{5,4},{6,5},{7,6},{8,11},{9,8},{10,9... | collective-permute-start | bytes 786440 | tf_op jit(solution)/shard_map/ppermute | solution.py:440
  208.9 2.4 shard_map.201
  211.3 4.8 %shard_map.202.refs_8_ = bf16[512,2048]{1,0:T(8,128)(2,1)} custom-call(s32[2]{0:T(128)S(1)} %get-tuple-element.94.refs_0_, f32[512,1024]{1,0:T(8,128)S(1)} %copy-done, f32[512,1024]{1,0:T(8,128)} %copy-done.32, f32[1,10240]{1,0:T(1,128)S(1)} %bitcast.17, f32[1,10240]{1,0:T(1,128)S(1)} %bitcast.18, f32[512,128]{1,0:T(8,128)S(1)} %get-tuple-element.101.cosine.refs_5_.refs_2_, ...), custom_call_target="tpu_custom_call" | custom-call | flops 536870912 | bytes 2097152 | tf_op jit(solution)/shard_map/pallas_call | solution.py:379
  220.0 5.3 %collective-permute-done.37.refs_2_ = bf16[256,512]{1,0:T(8,128)(2,1)S(1)} collective-permute-done((bf16[256,512]{1,0:T(8,128)(2,1)S(1)}, bf16[256,512]{1,0:T(8,128)(2,1)S(1)}, u32[]{:S(2)}, u32[]{:S(2)}) %collective-permute-start.37) | collective-permute-done | bytes 262176 | tf_op jit(solution)/shard_map/ppermute | solution.py:434
  226.8 6.3 %shard_map.204 = (f32[512,512]{1,0:T(8,128)}, f32[512,512]{1,0:T(8,128)}) custom-call(bf16[512,1024]{1,0:T(8,128)(2,1)} %collective-permute-done.32.refs_0_, bf16[512,1024]{1,0:T(8,128)(2,1)} %collective-permute-done.33.refs_1_, bf16[512,1024]{1,0:T(8,128)(2,1)} %collective-permute-done.34.refs_2_, bf16[512,1024]{1,0:T(8,128)(2,1)} %copy-done.8, ...), custom_call_target="tpu_custom_call" | custom-call | flops 3221225472 | bytes 11534336 | tf_op jit(solution)/shard_map/pallas_call | solution.py:240
  233.2 3.2 %shard_map.206 = f32[512,512]{1,0:T(8,128)} custom-call(bf16[512,1024]{1,0:T(8,128)(2,1)S(1)} %copy-done.4, bf16[256,512]{1,0:T(8,128)(2,1)S(1)} %collective-permute-done.17.refs_1_, bf16[256,512]{1,0:T(8,128)(2,1)S(1)} %collective-permute-done.37.refs_2_, bf16[256,512]{1,0:T(8,128)(2,1)S(1)} %collective-permute-done.38.refs_3_, ...), custom_call_target="tpu_custom_call" | custom-call | flops 536870912 | bytes 3145728 | tf_op jit(solution)/shard_map/pallas_call | solution.py:240
  239.8 7.1 %shard_map.208.refs_8_ = bf16[512,2048]{1,0:T(8,128)(2,1)} custom-call(s32[4]{0:T(128)S(1)} %broadcast_add_fusion.5.table, f32[512,1024]{1,0:T(8,128)S(1)} %copy-done.1, f32[512,1024]{1,0:T(8,128)} %collective-permute-done.53.other, f32[1,10240]{1,0:T(1,128)S(1)} %bitcast.19, f32[1,10240]{1,0:T(1,128)S(1)} %bitcast.20, ...), custom_call_target="tpu_custom_call", output_to_operand_aliasing={{}: (11, {})} | custom-call | flops 1073741824 | bytes 4194304 | tf_op jit(solution)/shard_map/pallas_call | solution.py:379
  247.0 4.8 %shard_map.209 = bf16[512,2048]{1,0:T(8,128)(2,1)} custom-call(s32[2]{0:T(128)S(1)} %broadcast_add_fusion.7.table, f32[512,512]{1,0:T(8,128)S(1)} %shard_map.205.own, f32[512,512]{1,0:T(8,128)} %collective-permute-done.52.other, f32[1,10240]{1,0:T(1,128)S(1)} %bitcast.21, f32[1,10240]{1,0:T(1,128)S(1)} %bitcast.22, ...), custom_call_target="tpu_custom_call", output_to_operand_aliasing={{}: (11, {})} | custom-call | flops 536870912 | bytes 2097152 | tf_op jit(solution)/shard_map/pallas_call | solution.py:379
  (222 shorter events, 67.7 us)
Async XLA Ops:
  6.7 24.7 %collective-permute-start = (bf16[256,1024]{1,0:T(8,128)(2,1)}, bf16[256,1024]{1,0:T(8,128)(2,1)S(1)}, u32[]{:S(2)}, u32[]{:S(2)}) collective-permute-start(bf16[256,1024]{1,0:T(8,128)(2,1)} %get-tuple-element.46), channel_id=1, source_target_pairs={{0,1},{1,2},{2,3},{3,0},{4,5},{5,6},{6,7},{7,4},{8,9},{9,10},{10,1... | collective-permute-start | bytes 1572872 | tf_op jit(solution)/shard_map/ppermute | solution.py:440
  13.1 19.9 %collective-permute-start.7 = (bf16[256,1536]{1,0:T(8,128)(2,1)S(1)}, bf16[256,1536]{1,0:T(8,128)(2,1)S(1)}, u32[]{:S(2)}, u32[]{:S(2)}) collective-permute-start(bf16[256,1536]{1,0:T(8,128)(2,1)S(1)} %shard_map.199.refs_6_.refs_8_), channel_id=1, source_target_pairs={{0,8},{4,20},{8,0},{12,28},{16,24},{20,4},{24,16},{28,12},{1,9},{5... | collective-permute-start | bytes 2359304 | tf_op jit(solution)/shard_map/ppermute | solution.py:434
  21.1 37.8 %collective-permute-start.12 = (bf16[256,1536]{1,0:T(8,128)(2,1)S(1)}, bf16[256,1536]{1,0:T(8,128)(2,1)}, u32[]{:S(2)}, u32[]{:S(2)}) collective-permute-start(bf16[256,1536]{1,0:T(8,128)(2,1)S(1)} %shard_map.199.refs_6_.refs_8_), channel_id=1, source_target_pairs={{0,16},{4,12},{8,24},{12,4},{16,0},{20,28},{24,8},{28,20},{1,17},{... | collective-permute-start | bytes 2359304 | tf_op jit(solution)/shard_map/ppermute | solution.py:434
  31.4 26.0 %collective-permute-start.11 = (bf16[256,1024]{1,0:T(8,128)(2,1)S(1)}, bf16[256,1024]{1,0:T(8,128)(2,1)}, u32[]{:S(2)}, u32[]{:S(2)}) collective-permute-start(bf16[256,1024]{1,0:T(8,128)(2,1)S(1)} %copy-done.26), channel_id=1, source_target_pairs={{0,2},{1,3},{2,0},{3,1},{4,6},{5,7},{6,4},{7,5},{8,10},{9,11},{10,... | collective-permute-start | bytes 1572872 | tf_op jit(solution)/shard_map/ppermute | solution.py:440
  33.0 38.0 %collective-permute-start.8 = (bf16[256,1536]{1,0:T(8,128)(2,1)S(1)}, bf16[256,1536]{1,0:T(8,128)(2,1)S(1)}, u32[]{:S(2)}, u32[]{:S(2)}) collective-permute-start(bf16[256,1536]{1,0:T(8,128)(2,1)S(1)} %collective-permute-done.7.refs_7_.refs_9_), channel_id=1, source_target_pairs={{0,16},{4,12},{8,24},{12,4},{16,0},{20,28},{24,8},{28,20},{1,17},{... | collective-permute-start | bytes 2359304 | tf_op jit(solution)/shard_map/ppermute | solution.py:434
  43.0 22.5 %collective-permute-start.13 = (bf16[256,1024]{1,0:T(8,128)(2,1)S(1)}, bf16[256,1024]{1,0:T(8,128)(2,1)S(1)}, u32[]{:S(2)}, u32[]{:S(2)}) collective-permute-start(bf16[256,1024]{1,0:T(8,128)(2,1)S(1)} %collective-permute-done.1.refs_9_), channel_id=1, source_target_pairs={{0,16},{4,12},{8,24},{12,4},{16,0},{20,28},{24,8},{28,20},{1,17},{... | collective-permute-start | bytes 1572872 | tf_op jit(solution)/shard_map/ppermute | solution.py:434
  49.0 17.8 %collective-permute-start.3 = (bf16[256,1024]{1,0:T(8,128)(2,1)S(1)}, bf16[256,1024]{1,0:T(8,128)(2,1)}, u32[]{:S(2)}, u32[]{:S(2)}) collective-permute-start(bf16[256,1024]{1,0:T(8,128)(2,1)S(1)} %collective-permute-done.refs_12_), channel_id=1, source_target_pairs={{0,8},{4,20},{8,0},{12,28},{16,24},{20,4},{24,16},{28,12},{1,9},{5... | collective-permute-start | bytes 1572872 | tf_op jit(solution)/shard_map/ppermute | solution.py:434
  66.3 16.8 %collective-permute-start.20 = (bf16[256,1024]{1,0:T(8,128)(2,1)S(1)}, bf16[256,1024]{1,0:T(8,128)(2,1)}, u32[]{:S(2)}, u32[]{:S(2)}) collective-permute-start(bf16[256,1024]{1,0:T(8,128)(2,1)S(1)} %get-tuple-element.59), channel_id=1, source_target_pairs={{0,1},{1,2},{2,3},{3,0},{4,5},{5,6},{6,7},{7,4},{8,9},{9,10},{10,1... | collective-permute-start | bytes 1572872 | tf_op jit(solution)/shard_map/ppermute | solution.py:440
  66.9 16.8 %collective-permute-start.14 = (bf16[256,1024]{1,0:T(8,128)(2,1)}, bf16[256,1024]{1,0:T(8,128)(2,1)}, u32[]{:S(2)}, u32[]{:S(2)}) collective-permute-start(bf16[256,1024]{1,0:T(8,128)(2,1)} %collective-permute-done.11.refs_16_), channel_id=1, source_target_pairs={{0,8},{4,20},{8,0},{12,28},{16,24},{20,4},{24,16},{28,12},{1,9},{5... | collective-permute-start | bytes 1572872 | tf_op jit(solution)/shard_map/ppermute | solution.py:434
  67.4 16.8 %collective-permute-start.21 = (bf16[256,1024]{1,0:T(8,128)(2,1)}, bf16[256,1024]{1,0:T(8,128)(2,1)S(1)}, u32[]{:S(2)}, u32[]{:S(2)}) collective-permute-start(bf16[256,1024]{1,0:T(8,128)(2,1)} %collective-permute-done.11.refs_16_), channel_id=1, source_target_pairs={{0,16},{4,12},{8,24},{12,4},{16,0},{20,28},{24,8},{28,20},{1,17},{... | collective-permute-start | bytes 1572872 | tf_op jit(solution)/shard_map/ppermute | solution.py:434
  69.4 20.8 %collective-permute-start.22 = (bf16[256,1024]{1,0:T(8,128)(2,1)}, bf16[256,1024]{1,0:T(8,128)(2,1)}, u32[]{:S(2)}, u32[]{:S(2)}) collective-permute-start(bf16[256,1024]{1,0:T(8,128)(2,1)} %collective-permute-done.3.refs_13_), channel_id=1, source_target_pairs={{0,16},{4,12},{8,24},{12,4},{16,0},{20,28},{24,8},{28,20},{1,17},{... | collective-permute-start | bytes 1572872 | tf_op jit(solution)/shard_map/ppermute | solution.py:434
  70.9 27.4 %collective-permute-start.4 = (bf16[256,1024]{1,0:T(8,128)(2,1)S(1)}, bf16[256,1024]{1,0:T(8,128)(2,1)S(1)}, u32[]{:S(2)}, u32[]{:S(2)}) collective-permute-start(bf16[256,1024]{1,0:T(8,128)(2,1)S(1)} %get-tuple-element.48), channel_id=1, source_target_pairs={{0,2},{1,3},{2,0},{3,1},{4,6},{5,7},{6,4},{7,5},{8,10},{9,11},{10,... | collective-permute-start | bytes 1572872 | tf_op jit(solution)/shard_map/ppermute | solution.py:440
  83.1 15.8 %collective-permute-start.9 = (bf16[256,1024]{1,0:T(8,128)(2,1)}, bf16[256,1024]{1,0:T(8,128)(2,1)}, u32[]{:S(2)}, u32[]{:S(2)}) collective-permute-start(bf16[256,1024]{1,0:T(8,128)(2,1)} %collective-permute-done.5.refs_20_), channel_id=1, source_target_pairs={{0,8},{4,20},{8,0},{12,28},{16,24},{20,4},{24,16},{28,12},{1,9},{5... | collective-permute-start | bytes 1572872 | tf_op jit(solution)/shard_map/ppermute | solution.py:434
  90.2 36.4 %collective-permute-start.23 = (bf16[256,1024]{1,0:T(8,128)(2,1)}, bf16[256,1024]{1,0:T(8,128)(2,1)}, u32[]{:S(2)}, u32[]{:S(2)}) collective-permute-start(bf16[256,1024]{1,0:T(8,128)(2,1)} %collective-permute-done.20.refs_12_), channel_id=1, source_target_pairs={{0,8},{4,20},{8,0},{12,28},{16,24},{20,4},{24,16},{28,12},{1,9},{5... | collective-permute-start | bytes 1572872 | tf_op jit(solution)/shard_map/ppermute | solution.py:434
  91.4 35.7 %collective-permute-start.27 = (bf16[256,1024]{1,0:T(8,128)(2,1)}, bf16[256,1024]{1,0:T(8,128)(2,1)}, u32[]{:S(2)}, u32[]{:S(2)}) collective-permute-start(bf16[256,1024]{1,0:T(8,128)(2,1)} %get-tuple-element.63), channel_id=1, source_target_pairs={{0,3},{1,0},{2,1},{3,2},{4,7},{5,4},{6,5},{7,6},{8,11},{9,8},{10,9... | collective-permute-start | bytes 1572872 | tf_op jit(solution)/shard_map/ppermute | solution.py:440
  93.7 32.9 %collective-permute-start.15 = (bf16[256,1024]{1,0:T(8,128)(2,1)}, bf16[256,1024]{1,0:T(8,128)(2,1)S(1)}, u32[]{:S(2)}, u32[]{:S(2)}) collective-permute-start(bf16[256,1024]{1,0:T(8,128)(2,1)} %collective-permute-done.14.refs_17_), channel_id=1, source_target_pairs={{0,16},{4,12},{8,24},{12,4},{16,0},{20,28},{24,8},{28,20},{1,17},{... | collective-permute-start | bytes 1572872 | tf_op jit(solution)/shard_map/ppermute | solution.py:434
  98.4 20.6 %collective-permute-start.10 = (bf16[256,1024]{1,0:T(8,128)(2,1)}, bf16[256,1024]{1,0:T(8,128)(2,1)S(1)}, u32[]{:S(2)}, u32[]{:S(2)}) collective-permute-start(bf16[256,1024]{1,0:T(8,128)(2,1)} %collective-permute-done.5.refs_20_), channel_id=1, source_target_pairs={{0,16},{4,12},{8,24},{12,4},{16,0},{20,28},{24,8},{28,20},{1,17},{... | collective-permute-start | bytes 1572872 | tf_op jit(solution)/shard_map/ppermute | solution.py:434
  98.9 28.6 %collective-permute-start.28 = (bf16[256,1024]{1,0:T(8,128)(2,1)}, bf16[256,1024]{1,0:T(8,128)(2,1)S(1)}, u32[]{:S(2)}, u32[]{:S(2)}) collective-permute-start(bf16[256,1024]{1,0:T(8,128)(2,1)} %collective-permute-done.20.refs_12_), channel_id=1, source_target_pairs={{0,16},{4,12},{8,24},{12,4},{16,0},{20,28},{24,8},{28,20},{1,17},{... | collective-permute-start | bytes 1572872 | tf_op jit(solution)/shard_map/ppermute | solution.py:434
  119.0 20.6 %collective-permute-start.32 = (bf16[512,1024]{1,0:T(8,128)(2,1)}, bf16[512,1024]{1,0:T(8,128)(2,1)}, u32[]{:S(2)}, u32[]{:S(2)}) collective-permute-start(bf16[512,1024]{1,0:T(8,128)(2,1)} %get-tuple-element.65), channel_id=1, source_target_pairs={{0,4},{4,0},{8,12},{12,8},{16,20},{20,16},{24,28},{28,24},{1,5},{5... | collective-permute-start | bytes 3145736 | tf_op jit(solution)/shard_map/ppermute | solution.py:437
  126.7 18.6 %collective-permute-start.34 = (bf16[512,1024]{1,0:T(8,128)(2,1)}, bf16[512,1024]{1,0:T(8,128)(2,1)}, u32[]{:S(2)}, u32[]{:S(2)}) collective-permute-start(bf16[512,1024]{1,0:T(8,128)(2,1)} %get-tuple-element.67), channel_id=1, source_target_pairs={{0,4},{4,0},{8,12},{12,8},{16,20},{20,16},{24,28},{28,24},{1,5},{5... | collective-permute-start | bytes 3145736 | tf_op jit(solution)/shard_map/ppermute | solution.py:437
  127.1 18.4 %collective-permute-start.35 = (bf16[512,1024]{1,0:T(8,128)(2,1)}, bf16[512,1024]{1,0:T(8,128)(2,1)S(1)}, u32[]{:S(2)}, u32[]{:S(2)}) collective-permute-start(bf16[512,1024]{1,0:T(8,128)(2,1)} %get-tuple-element.68), channel_id=1, source_target_pairs={{0,4},{4,0},{8,12},{12,8},{16,20},{20,16},{24,28},{28,24},{1,5},{5... | collective-permute-start | bytes 3145736 | tf_op jit(solution)/shard_map/ppermute | solution.py:437
  137.9 28.6 %collective-permute-start.16 = (bf16[256,1024]{1,0:T(8,128)(2,1)S(1)}, bf16[256,1024]{1,0:T(8,128)(2,1)S(1)}, u32[]{:S(2)}, u32[]{:S(2)}) collective-permute-start(bf16[256,1024]{1,0:T(8,128)(2,1)S(1)} %collective-permute-done.4.refs_16_), channel_id=1, source_target_pairs={{0,8},{4,20},{8,0},{12,28},{16,24},{20,4},{24,16},{28,12},{1,9},{5... | collective-permute-start | bytes 1572872 | tf_op jit(solution)/shard_map/ppermute | solution.py:434
  139.5 27.0 %collective-permute-start.19 = (bf16[256,1024]{1,0:T(8,128)(2,1)S(1)}, bf16[256,1024]{1,0:T(8,128)(2,1)S(1)}, u32[]{:S(2)}, u32[]{:S(2)}) collective-permute-start(bf16[256,1024]{1,0:T(8,128)(2,1)S(1)} %collective-permute-done.4.refs_16_), channel_id=1, source_target_pairs={{0,16},{4,12},{8,24},{12,4},{16,0},{20,28},{24,8},{28,20},{1,17},{... | collective-permute-start | bytes 1572872 | tf_op jit(solution)/shard_map/ppermute | solution.py:434
  140.0 24.9 %collective-permute-start.18 = (bf16[256,512]{1,0:T(8,128)(2,1)}, bf16[256,512]{1,0:T(8,128)(2,1)S(1)}, u32[]{:S(2)}, u32[]{:S(2)}) collective-permute-start(bf16[256,512]{1,0:T(8,128)(2,1)} %copy-done.31), channel_id=1, source_target_pairs={{0,1},{1,2},{2,3},{3,0},{4,5},{5,6},{6,7},{7,4},{8,9},{9,10},{10,1... | collective-permute-start | bytes 786440 | tf_op jit(solution)/shard_map/ppermute | solution.py:440
  145.3 23.4 %collective-permute-start.24 = (bf16[256,1024]{1,0:T(8,128)(2,1)}, bf16[256,1024]{1,0:T(8,128)(2,1)S(1)}, u32[]{:S(2)}, u32[]{:S(2)}) collective-permute-start(bf16[256,1024]{1,0:T(8,128)(2,1)} %collective-permute-done.23.refs_13_), channel_id=1, source_target_pairs={{0,16},{4,12},{8,24},{12,4},{16,0},{20,28},{24,8},{28,20},{1,17},{... | collective-permute-start | bytes 1572872 | tf_op jit(solution)/shard_map/ppermute | solution.py:434
  145.5 21.5 %collective-permute-start.30 = (bf16[256,1024]{1,0:T(8,128)(2,1)}, bf16[256,1024]{1,0:T(8,128)(2,1)S(1)}, u32[]{:S(2)}, u32[]{:S(2)}) collective-permute-start(bf16[256,1024]{1,0:T(8,128)(2,1)} %collective-permute-done.27.refs_20_), channel_id=1, source_target_pairs={{0,8},{4,20},{8,0},{12,28},{16,24},{20,4},{24,16},{28,12},{1,9},{5... | collective-permute-start | bytes 1572872 | tf_op jit(solution)/shard_map/ppermute | solution.py:434
  166.5 41.1 %collective-permute-start.36 = (f32[512,1024]{1,0:T(8,128)}, f32[512,1024]{1,0:T(8,128)S(1)}, u32[]{:S(2)}, u32[]{:S(2)}) collective-permute-start(f32[512,1024]{1,0:T(8,128)} %get-tuple-element.73), channel_id=1, source_target_pairs={{0,4},{4,0},{8,12},{12,8},{16,20},{20,16},{24,28},{28,24},{1,5},{5... | collective-permute-start | bytes 6291464 | tf_op jit(solution)/shard_map/ppermute | solution.py:437
  166.5 16.3 %collective-permute-start.43 = (bf16[256,1024]{1,0:T(8,128)(2,1)S(1)}, bf16[256,1024]{1,0:T(8,128)(2,1)S(1)}, u32[]{:S(2)}, u32[]{:S(2)}) collective-permute-start(bf16[256,1024]{1,0:T(8,128)(2,1)S(1)} %collective-permute-done.16.refs_17_), channel_id=1, source_target_pairs={{0,16},{4,12},{8,24},{12,4},{16,0},{20,28},{24,8},{28,20},{1,17},{... | collective-permute-start | bytes 1572872 | tf_op jit(solution)/shard_map/ppermute | solution.py:434
  167.1 21.3 %collective-permute-start.31 = (bf16[256,1024]{1,0:T(8,128)(2,1)S(1)}, bf16[256,1024]{1,0:T(8,128)(2,1)S(1)}, u32[]{:S(2)}, u32[]{:S(2)}) collective-permute-start(bf16[256,1024]{1,0:T(8,128)(2,1)S(1)} %collective-permute-done.30.refs_21_), channel_id=1, source_target_pairs={{0,16},{4,12},{8,24},{12,4},{16,0},{20,28},{24,8},{28,20},{1,17},{... | collective-permute-start | bytes 1572872 | tf_op jit(solution)/shard_map/ppermute | solution.py:434
  168.7 35.2 %collective-permute-start.41 = (bf16[256,512]{1,0:T(8,128)(2,1)S(1)}, bf16[256,512]{1,0:T(8,128)(2,1)S(1)}, u32[]{:S(2)}, u32[]{:S(2)}) collective-permute-start(bf16[256,512]{1,0:T(8,128)(2,1)S(1)} %copy-done.30), channel_id=1, source_target_pairs={{0,2},{1,3},{2,0},{3,1},{4,6},{5,7},{6,4},{7,5},{8,10},{9,11},{10,... | collective-permute-start | bytes 786440 | tf_op jit(solution)/shard_map/ppermute | solution.py:440
  174.4 32.2 %collective-permute-start.25 = (bf16[256,512]{1,0:T(8,128)(2,1)S(1)}, bf16[256,512]{1,0:T(8,128)(2,1)S(1)}, u32[]{:S(2)}, u32[]{:S(2)}) collective-permute-start(bf16[256,512]{1,0:T(8,128)(2,1)S(1)} %collective-permute-done.18.refs_10_), channel_id=1, source_target_pairs={{0,8},{4,20},{8,0},{12,28},{16,24},{20,4},{24,16},{28,12},{1,9},{5... | collective-permute-start | bytes 786440 | tf_op jit(solution)/shard_map/ppermute | solution.py:434
  202.2 37.6 %collective-permute-start.53 = (f32[512,1024]{1,0:T(8,128)}, f32[512,1024]{1,0:T(8,128)}, u32[]{:S(2)}, u32[]{:S(2)}) collective-permute-start(f32[512,1024]{1,0:T(8,128)} %get-tuple-element.83), channel_id=1, source_target_pairs={{0,4},{4,0},{8,12},{12,8},{16,20},{20,16},{24,28},{28,24},{1,5},{5... | collective-permute-start | bytes 6291464 | tf_op jit(solution)/shard_map/ppermute | solution.py:437
  (70 other events, 792.7 us)

commit v3 on v2

--- a/solution.py
+++ b/solution.py
@@ -213,11 +213,13 @@
                 )
             )
         copies.append(own)
-        for copy in own:
-            copy.start()
+    for copy in [c for own in copies[:2] for c in own]:
+        copy.start()
     for r in range(runs):
         for copy in copies[r]:
             copy.wait()
+        for copy in copies[r + 2] if r + 2 < runs else []:
+            copy.start()
         for n, out in enumerate(outs):
             part = jnp.dot(x_held[n, r], w_held[r], preferred_element_type=jnp.float32)
             if r > 0:

time: 253 us -> 253 us (level)
  no operation moved by 1% of the time
where the time goes in v3:
time: 253 us; the launch traced here: 252 us
  Pallas kernels  88.9 us (35%)
  waiting for transfers between devices  76.8 us (30%)
  starting transfers between devices  68.9 us (27%)
  local copies, waits for them, and re-layouts  13.2 us (5%)
  other arithmetic  3.19 us (1%)
    ppermute x33, waiting for transfers between devices, gather_step(): lax.ppermute(value, 'rep', [(r, r ^ bit_of(step, r % 2)) for r in range(n...  48.8 us
    pallas_call x5, Pallas kernels, product(): pl.pallas_call(functools.partial(product_kernel, tuple(offsets), runs, co...  37.6 us
    ppermute x33, starting transfers between devices, gather_step(): lax.ppermute(value, 'rep', [(r, r ^ bit_of(step, r % 2)) for r in range(n...  34.4 us
    ppermute x9, waiting for transfers between devices, to_server(): lax.ppermute(value, 'tp', [(t, (t + shift) % n_tp) for t in range(n_tp)])  23.2 us
    ppermute x9, starting transfers between devices, to_server(): lax.ppermute(value, 'tp', [(t, (t + shift) % n_tp) for t in range(n_tp)])  20.4 us
    pallas_call x5, Pallas kernels, restore(): pl.pallas_call(functools.partial(restore_kernel, views), grid_spec=pltpu....  18.1 us
    pallas_call x3, Pallas kernels, attention(): pl.pallas_call(body, grid_spec=pltpu.PrefetchScalarGridSpec(num_scalar_pr...  16.8 us
    unnamed x97, local copies, waits for them, and re-layouts  12.8 us
  transfers between devices with their start and end apart: 54, of which 16 were waited for; matrix products, arithmetic and copies ran while one was open for 1% of the time, Pallas kernels for 31%

profile of v3, /device:TPU:0, one launch (start us, length us, event | category | flops | bytes accessed | tf_op | source)
XLA Modules:
  0.0 252.2 jit_solution(20763173968932597)
XLA Ops:
  2.0 4.7 %shard_map.197 = (bf16[256,1024]{1,0:T(8,128)(2,1)}, bf16[256,1024]{1,0:T(8,128)(2,1)S(1)}, bf16[256,1024]{1,0:T(8,128)(2,1)S(1)}) custom-call(s32[3,4]{1,0:T(4,128)S(1)} %get-tuple-element.97.table, bf16[256,10240]{1,0:T(8,128)(2,1)} %weight.1, bf16[256,10240]{1,0:T(8,128)(2,1)} %weight.1, bf16[256,10240]{1,0:T(8,128)(2,1)} %weight.1), custom_call_target="tpu_custom_call" | custom-call | flops 12582912 | bytes 3145728 | tf_op jit(solution)/shard_map/pallas_call | solution.py:79
  6.7 3.0 %collective-permute-start = (bf16[256,1024]{1,0:T(8,128)(2,1)}, bf16[256,1024]{1,0:T(8,128)(2,1)S(1)}, u32[]{:S(2)}, u32[]{:S(2)}) collective-permute-start(bf16[256,1024]{1,0:T(8,128)(2,1)} %get-tuple-element.46), channel_id=1, source_target_pairs={{0,1},{1,2},{2,3},{3,0},{4,5},{5,6},{6,7},{7,4},{8,9},{9,10},{10,1... | collective-permute-start | bytes 1572872 | tf_op jit(solution)/shard_map/ppermute | solution.py:442
  9.8 3.3 %shard_map.199.refs_6_.refs_8_ = bf16[256,1536]{1,0:T(8,128)(2,1)S(1)} custom-call(s32[1,6]{1,0:T(1,128)S(1)} %add_bitcast_fusion.table, bf16[256,10240]{1,0:T(8,128)(2,1)} %weight.1, bf16[256,10240]{1,0:T(8,128)(2,1)} %weight.1), custom_call_target="tpu_custom_call" | custom-call | flops 6291456 | bytes 1572864 | tf_op jit(solution)/shard_map/pallas_call | solution.py:79
  14.7 4.8 %shard_map.203 = f32[8,128]{1,0:T(8,128)S(1)} custom-call(bf16[256,10240]{1,0:T(8,128)(2,1)} %weight.1, s32[1]{0:T(128)} %constant.137.clone.fence), custom_call_target="tpu_custom_call" | custom-call | flops 5242880 | bytes 5242880 | tf_op jit(solution)/shard_map/pallas_call | solution.py:118
  23.0 2.7 %collective-permute-start.45 = (bf16[4,80]{1,0:T(4,128)(2,1)S(1)}, bf16[4,80]{1,0:T(4,128)(2,1)S(1)}, u32[]{:S(2)}, u32[]{:S(2)}) collective-permute-start(bf16[4,80]{1,0:T(4,128)(2,1)S(1)} %pad_maximum_fusion.4), channel_id=1, source_target_pairs={{0,2},{1,3},{2,0},{3,1},{4,6},{5,7},{6,4},{7,5},{8,10},{9,11},{10,... | collective-permute-start | bytes 1928 | tf_op jit(solution)/shard_map/ppermute | solution.py:410
  25.7 2.3 shard_map.198.refs_8_
  33.5 9.5 %collective-permute-done.1.refs_9_ = bf16[256,1024]{1,0:T(8,128)(2,1)S(1)} collective-permute-done((bf16[256,1024]{1,0:T(8,128)(2,1)S(1)}, bf16[256,1024]{1,0:T(8,128)(2,1)S(1)}, u32[]{:S(2)}, u32[]{:S(2)}) %collective-permute-start.1) | collective-permute-done | bytes 524320 | tf_op jit(solution)/shard_map/ppermute | solution.py:436
  45.8 3.2 %collective-permute-done.47 = bf16[16,80]{1,0:T(8,128)(2,1)S(1)} collective-permute-done((bf16[16,80]{1,0:T(8,128)(2,1)S(1)}, bf16[16,80]{1,0:T(8,128)(2,1)S(1)}, u32[]{:S(2)}, u32[]{:S(2)}) %collective-permute-start.47) | collective-permute-done | bytes 2592 | tf_op jit(solution)/shard_map/ppermute | solution.py:410
  49.6 7.8 %collective-permute-done.11.refs_16_ = bf16[256,1024]{1,0:T(8,128)(2,1)} collective-permute-done((bf16[256,1024]{1,0:T(8,128)(2,1)S(1)}, bf16[256,1024]{1,0:T(8,128)(2,1)}, u32[]{:S(2)}, u32[]{:S(2)}) %collective-permute-start.11) | collective-permute-done | bytes 524320 | tf_op jit(solution)/shard_map/ppermute | solution.py:442
  60.4 5.1 %shard_map.196 = (bf16[256,1024]{1,0:T(8,128)(2,1)S(1)}, bf16[256,1024]{1,0:T(8,128)(2,1)S(1)}, bf16[256,1024]{1,0:T(8,128)(2,1)}) custom-call(s32[3,4]{1,0:T(4,128)S(1)} %get-tuple-element.98.table, bf16[256,10240]{1,0:T(8,128)(2,1)} %weight.1, bf16[256,10240]{1,0:T(8,128)(2,1)} %weight.1, bf16[256,10240]{1,0:T(8,128)(2,1)} %weight.1), custom_call_target="tpu_custom_call" | custom-call | flops 12582912 | bytes 3145728 | tf_op jit(solution)/shard_map/pallas_call | solution.py:79
  70.9 12.2 %collective-permute-done.20.refs_12_ = bf16[256,1024]{1,0:T(8,128)(2,1)} collective-permute-done((bf16[256,1024]{1,0:T(8,128)(2,1)S(1)}, bf16[256,1024]{1,0:T(8,128)(2,1)}, u32[]{:S(2)}, u32[]{:S(2)}) %collective-permute-start.20) | collective-permute-done | bytes 524320 | tf_op jit(solution)/shard_map/ppermute | solution.py:442
  84.3 6.0 %collective-permute-done.22.refs_15_ = bf16[256,1024]{1,0:T(8,128)(2,1)} collective-permute-done((bf16[256,1024]{1,0:T(8,128)(2,1)}, bf16[256,1024]{1,0:T(8,128)(2,1)}, u32[]{:S(2)}, u32[]{:S(2)}) %collective-permute-start.22) | collective-permute-done | bytes 524320 | tf_op jit(solution)/shard_map/ppermute | solution.py:436
  95.2 3.1 %collective-permute-done.4.refs_16_ = bf16[256,1024]{1,0:T(8,128)(2,1)S(1)} collective-permute-done((bf16[256,1024]{1,0:T(8,128)(2,1)S(1)}, bf16[256,1024]{1,0:T(8,128)(2,1)S(1)}, u32[]{:S(2)}, u32[]{:S(2)}) %collective-permute-start.4) | collective-permute-done | bytes 524320 | tf_op jit(solution)/shard_map/ppermute | solution.py:442
  100.6 9.3 %shard_map.194 = (bf16[512,1024]{1,0:T(8,128)(2,1)S(1)}, bf16[512,1024]{1,0:T(8,128)(2,1)S(1)}, bf16[512,1024]{1,0:T(8,128)(2,1)S(1)}, bf16[512,1024]{1,0:T(8,12...) custom-call(s32[8,4]{1,0:T(8,128)S(1)} %pad_add_fusion.table, ...), custom_call_target="tpu_custom_call" | custom-call | flops 25165824 | bytes 16777216 | tf_op jit(solution)/shard_map/pallas_call | solution.py:170
  111.8 7.1 %collective-permute-done.10.refs_22_ = bf16[256,1024]{1,0:T(8,128)(2,1)S(1)} collective-permute-done((bf16[256,1024]{1,0:T(8,128)(2,1)}, bf16[256,1024]{1,0:T(8,128)(2,1)S(1)}, u32[]{:S(2)}, u32[]{:S(2)}) %collective-permute-start.10) | collective-permute-done | bytes 524320 | tf_op jit(solution)/shard_map/ppermute | solution.py:436
  119.0 7.6 %collective-permute-start.32 = (bf16[512,1024]{1,0:T(8,128)(2,1)}, bf16[512,1024]{1,0:T(8,128)(2,1)}, u32[]{:S(2)}, u32[]{:S(2)}) collective-permute-start(bf16[512,1024]{1,0:T(8,128)(2,1)} %get-tuple-element.65), channel_id=1, source_target_pairs={{0,4},{4,0},{8,12},{12,8},{16,20},{20,16},{24,28},{28,24},{1,5},{5... | collective-permute-start | bytes 3145736 | tf_op jit(solution)/shard_map/ppermute | solution.py:439
  129.2 2.8 %shard_map.195 = (bf16[256,512]{1,0:T(8,128)(2,1)S(1)}, bf16[256,512]{1,0:T(8,128)(2,1)S(1)}, bf16[256,512]{1,0:T(8,128)(2,1)S(1)}) custom-call(s32[3,2]{1,0:T(4,128)S(1)} %broadcast_add_fusion.2.table, bf16[256,10240]{1,0:T(8,128)(2,1)} %weight.1, bf16[256,10240]{1,0:T(8,128)(2,1)} %weight.1, bf16[256,10240]{1,0:T(8,128)(2,1)} %weight.1), custom_call_target="tpu_custom_call" | custom-call | flops 6291456 | bytes 1572864 | tf_op jit(solution)/shard_map/pallas_call | solution.py:79
  133.4 4.5 %collective-permute-done.29.refs_23_ = bf16[256,1024]{1,0:T(8,128)(2,1)} collective-permute-done((bf16[256,1024]{1,0:T(8,128)(2,1)}, bf16[256,1024]{1,0:T(8,128)(2,1)}, u32[]{:S(2)}, u32[]{:S(2)}) %collective-permute-start.29) | collective-permute-done | bytes 524320 | tf_op jit(solution)/shard_map/ppermute | solution.py:436
  140.0 5.2 %collective-permute-start.18 = (bf16[256,512]{1,0:T(8,128)(2,1)}, bf16[256,512]{1,0:T(8,128)(2,1)S(1)}, u32[]{:S(2)}, u32[]{:S(2)}) collective-permute-start(bf16[256,512]{1,0:T(8,128)(2,1)} %copy-done.31), channel_id=1, source_target_pairs={{0,1},{1,2},{2,3},{3,0},{4,5},{5,6},{6,7},{7,4},{8,9},{9,10},{10,1... | collective-permute-start | bytes 786440 | tf_op jit(solution)/shard_map/ppermute | solution.py:442
  152.5 12.4 %shard_map.200 = (f32[512,1024]{1,0:T(8,128)}, f32[512,1024]{1,0:T(8,128)}) custom-call(bf16[512,1024]{1,0:T(8,128)(2,1)} %collective-permute-done.32.refs_0_, bf16[512,1024]{1,0:T(8,128)(2,1)} %collective-permute-done.33.refs_1_, bf16[512,1024]{1,0:T(8,128)(2,1)} %collective-permute-done.34.refs_2_, bf16[512,1024]{1,0:T(8,128)(2,1)} %copy-done.3, ...), custom_call_target="tpu_custom_call" | custom-call | flops 8589934592 | bytes 20971520 | tf_op jit(solution)/shard_map/pallas_call | solution.py:242
  168.7 3.6 %collective-permute-start.41 = (bf16[256,512]{1,0:T(8,128)(2,1)S(1)}, bf16[256,512]{1,0:T(8,128)(2,1)S(1)}, u32[]{:S(2)}, u32[]{:S(2)}) collective-permute-start(bf16[256,512]{1,0:T(8,128)(2,1)S(1)} %copy-done.30), channel_id=1, source_target_pairs={{0,2},{1,3},{2,0},{3,1},{4,6},{5,7},{6,4},{7,5},{8,10},{9,11},{10,... | collective-permute-start | bytes 786440 | tf_op jit(solution)/shard_map/ppermute | solution.py:442
  175.3 7.5 %collective-permute-done.43.refs_19_ = bf16[256,1024]{1,0:T(8,128)(2,1)S(1)} collective-permute-done((bf16[256,1024]{1,0:T(8,128)(2,1)S(1)}, bf16[256,1024]{1,0:T(8,128)(2,1)S(1)}, u32[]{:S(2)}, u32[]{:S(2)}) %collective-permute-start.43) | collective-permute-done | bytes 524320 | tf_op jit(solution)/shard_map/ppermute | solution.py:436
  182.8 5.6 %collective-permute-done.31.refs_23_ = bf16[256,1024]{1,0:T(8,128)(2,1)S(1)} collective-permute-done((bf16[256,1024]{1,0:T(8,128)(2,1)S(1)}, bf16[256,1024]{1,0:T(8,128)(2,1)S(1)}, u32[]{:S(2)}, u32[]{:S(2)}) %collective-permute-start.31) | collective-permute-done | bytes 524320 | tf_op jit(solution)/shard_map/ppermute | solution.py:436
  189.2 13.3 %shard_map.207 = (f32[512,1024]{1,0:T(8,128)}, f32[512,1024]{1,0:T(8,128)}) custom-call(bf16[512,1024]{1,0:T(8,128)(2,1)} %collective-permute-done.32.refs_0_, bf16[512,1024]{1,0:T(8,128)(2,1)} %collective-permute-done.33.refs_1_, bf16[512,1024]{1,0:T(8,128)(2,1)} %collective-permute-done.34.refs_2_, bf16[512,1024]{1,0:T(8,128)(2,1)} %copy-done.3, ...), custom_call_target="tpu_custom_call" | custom-call | flops 8589934592 | bytes 20971520 | tf_op jit(solution)/shard_map/pallas_call | solution.py:242
  204.2 2.6 %collective-permute-start.17 = (bf16[256,512]{1,0:T(8,128)(2,1)S(1)}, bf16[256,512]{1,0:T(8,128)(2,1)S(1)}, u32[]{:S(2)}, u32[]{:S(2)}) collective-permute-start(bf16[256,512]{1,0:T(8,128)(2,1)S(1)} %copy-done.28), channel_id=1, source_target_pairs={{0,3},{1,0},{2,1},{3,2},{4,7},{5,4},{6,5},{7,6},{8,11},{9,8},{10,9... | collective-permute-start | bytes 786440 | tf_op jit(solution)/shard_map/ppermute | solution.py:442
  209.2 2.4 shard_map.201
  211.6 4.8 %shard_map.202.refs_8_ = bf16[512,2048]{1,0:T(8,128)(2,1)} custom-call(s32[2]{0:T(128)S(1)} %get-tuple-element.94.refs_0_, f32[512,1024]{1,0:T(8,128)S(1)} %copy-done, f32[512,1024]{1,0:T(8,128)} %copy-done.32, f32[1,10240]{1,0:T(1,128)S(1)} %bitcast.17, f32[1,10240]{1,0:T(1,128)S(1)} %bitcast.18, f32[512,128]{1,0:T(8,128)S(1)} %get-tuple-element.101.cosine.refs_5_.refs_2_, ...), custom_call_target="tpu_custom_call" | custom-call | flops 536870912 | bytes 2097152 | tf_op jit(solution)/shard_map/pallas_call | solution.py:381
  220.3 5.4 %collective-permute-done.37.refs_2_ = bf16[256,512]{1,0:T(8,128)(2,1)S(1)} collective-permute-done((bf16[256,512]{1,0:T(8,128)(2,1)S(1)}, bf16[256,512]{1,0:T(8,128)(2,1)S(1)}, u32[]{:S(2)}, u32[]{:S(2)}) %collective-permute-start.37) | collective-permute-done | bytes 262176 | tf_op jit(solution)/shard_map/ppermute | solution.py:436
  227.2 6.4 %shard_map.204 = (f32[512,512]{1,0:T(8,128)}, f32[512,512]{1,0:T(8,128)}) custom-call(bf16[512,1024]{1,0:T(8,128)(2,1)} %collective-permute-done.32.refs_0_, bf16[512,1024]{1,0:T(8,128)(2,1)} %collective-permute-done.33.refs_1_, bf16[512,1024]{1,0:T(8,128)(2,1)} %collective-permute-done.34.refs_2_, bf16[512,1024]{1,0:T(8,128)(2,1)} %copy-done.8, ...), custom_call_target="tpu_custom_call" | custom-call | flops 3221225472 | bytes 11534336 | tf_op jit(solution)/shard_map/pallas_call | solution.py:242
  233.6 3.2 %shard_map.206 = f32[512,512]{1,0:T(8,128)} custom-call(bf16[512,1024]{1,0:T(8,128)(2,1)S(1)} %copy-done.4, bf16[256,512]{1,0:T(8,128)(2,1)S(1)} %collective-permute-done.17.refs_1_, bf16[256,512]{1,0:T(8,128)(2,1)S(1)} %collective-permute-done.37.refs_2_, bf16[256,512]{1,0:T(8,128)(2,1)S(1)} %collective-permute-done.38.refs_3_, ...), custom_call_target="tpu_custom_call" | custom-call | flops 536870912 | bytes 3145728 | tf_op jit(solution)/shard_map/pallas_call | solution.py:242
  240.3 7.1 %shard_map.208.refs_8_ = bf16[512,2048]{1,0:T(8,128)(2,1)} custom-call(s32[4]{0:T(128)S(1)} %broadcast_add_fusion.5.table, f32[512,1024]{1,0:T(8,128)S(1)} %copy-done.1, f32[512,1024]{1,0:T(8,128)} %collective-permute-done.53.other, f32[1,10240]{1,0:T(1,128)S(1)} %bitcast.19, f32[1,10240]{1,0:T(1,128)S(1)} %bitcast.20, ...), custom_call_target="tpu_custom_call", output_to_operand_aliasing={{}: (11, {})} | custom-call | flops 1073741824 | bytes 4194304 | tf_op jit(solution)/shard_map/pallas_call | solution.py:381
  247.4 4.8 %shard_map.209 = bf16[512,2048]{1,0:T(8,128)(2,1)} custom-call(s32[2]{0:T(128)S(1)} %broadcast_add_fusion.7.table, f32[512,512]{1,0:T(8,128)S(1)} %shard_map.205.own, f32[512,512]{1,0:T(8,128)} %collective-permute-done.52.other, f32[1,10240]{1,0:T(1,128)S(1)} %bitcast.21, f32[1,10240]{1,0:T(1,128)S(1)} %bitcast.22, ...), custom_call_target="tpu_custom_call", output_to_operand_aliasing={{}: (11, {})} | custom-call | flops 536870912 | bytes 2097152 | tf_op jit(solution)/shard_map/pallas_call | solution.py:381
  (222 shorter events, 67.7 us)
Async XLA Ops:
  6.7 24.7 %collective-permute-start = (bf16[256,1024]{1,0:T(8,128)(2,1)}, bf16[256,1024]{1,0:T(8,128)(2,1)S(1)}, u32[]{:S(2)}, u32[]{:S(2)}) collective-permute-start(bf16[256,1024]{1,0:T(8,128)(2,1)} %get-tuple-element.46), channel_id=1, source_target_pairs={{0,1},{1,2},{2,3},{3,0},{4,5},{5,6},{6,7},{7,4},{8,9},{9,10},{10,1... | collective-permute-start | bytes 1572872 | tf_op jit(solution)/shard_map/ppermute | solution.py:442
  13.1 19.9 %collective-permute-start.7 = (bf16[256,1536]{1,0:T(8,128)(2,1)S(1)}, bf16[256,1536]{1,0:T(8,128)(2,1)S(1)}, u32[]{:S(2)}, u32[]{:S(2)}) collective-permute-start(bf16[256,1536]{1,0:T(8,128)(2,1)S(1)} %shard_map.199.refs_6_.refs_8_), channel_id=1, source_target_pairs={{0,8},{4,20},{8,0},{12,28},{16,24},{20,4},{24,16},{28,12},{1,9},{5... | collective-permute-start | bytes 2359304 | tf_op jit(solution)/shard_map/ppermute | solution.py:436
  21.1 37.8 %collective-permute-start.12 = (bf16[256,1536]{1,0:T(8,128)(2,1)S(1)}, bf16[256,1536]{1,0:T(8,128)(2,1)}, u32[]{:S(2)}, u32[]{:S(2)}) collective-permute-start(bf16[256,1536]{1,0:T(8,128)(2,1)S(1)} %shard_map.199.refs_6_.refs_8_), channel_id=1, source_target_pairs={{0,16},{4,12},{8,24},{12,4},{16,0},{20,28},{24,8},{28,20},{1,17},{... | collective-permute-start | bytes 2359304 | tf_op jit(solution)/shard_map/ppermute | solution.py:436
  31.4 26.0 %collective-permute-start.11 = (bf16[256,1024]{1,0:T(8,128)(2,1)S(1)}, bf16[256,1024]{1,0:T(8,128)(2,1)}, u32[]{:S(2)}, u32[]{:S(2)}) collective-permute-start(bf16[256,1024]{1,0:T(8,128)(2,1)S(1)} %copy-done.26), channel_id=1, source_target_pairs={{0,2},{1,3},{2,0},{3,1},{4,6},{5,7},{6,4},{7,5},{8,10},{9,11},{10,... | collective-permute-start | bytes 1572872 | tf_op jit(solution)/shard_map/ppermute | solution.py:442
  33.0 38.0 %collective-permute-start.8 = (bf16[256,1536]{1,0:T(8,128)(2,1)S(1)}, bf16[256,1536]{1,0:T(8,128)(2,1)S(1)}, u32[]{:S(2)}, u32[]{:S(2)}) collective-permute-start(bf16[256,1536]{1,0:T(8,128)(2,1)S(1)} %collective-permute-done.7.refs_7_.refs_9_), channel_id=1, source_target_pairs={{0,16},{4,12},{8,24},{12,4},{16,0},{20,28},{24,8},{28,20},{1,17},{... | collective-permute-start | bytes 2359304 | tf_op jit(solution)/shard_map/ppermute | solution.py:436
  43.0 22.5 %collective-permute-start.13 = (bf16[256,1024]{1,0:T(8,128)(2,1)S(1)}, bf16[256,1024]{1,0:T(8,128)(2,1)S(1)}, u32[]{:S(2)}, u32[]{:S(2)}) collective-permute-start(bf16[256,1024]{1,0:T(8,128)(2,1)S(1)} %collective-permute-done.1.refs_9_), channel_id=1, source_target_pairs={{0,16},{4,12},{8,24},{12,4},{16,0},{20,28},{24,8},{28,20},{1,17},{... | collective-permute-start | bytes 1572872 | tf_op jit(solution)/shard_map/ppermute | solution.py:436
  49.0 17.8 %collective-permute-start.3 = (bf16[256,1024]{1,0:T(8,128)(2,1)S(1)}, bf16[256,1024]{1,0:T(8,128)(2,1)}, u32[]{:S(2)}, u32[]{:S(2)}) collective-permute-start(bf16[256,1024]{1,0:T(8,128)(2,1)S(1)} %collective-permute-done.refs_12_), channel_id=1, source_target_pairs={{0,8},{4,20},{8,0},{12,28},{16,24},{20,4},{24,16},{28,12},{1,9},{5... | collective-permute-start | bytes 1572872 | tf_op jit(solution)/shard_map/ppermute | solution.py:436
  66.3 16.8 %collective-permute-start.20 = (bf16[256,1024]{1,0:T(8,128)(2,1)S(1)}, bf16[256,1024]{1,0:T(8,128)(2,1)}, u32[]{:S(2)}, u32[]{:S(2)}) collective-permute-start(bf16[256,1024]{1,0:T(8,128)(2,1)S(1)} %get-tuple-element.59), channel_id=1, source_target_pairs={{0,1},{1,2},{2,3},{3,0},{4,5},{5,6},{6,7},{7,4},{8,9},{9,10},{10,1... | collective-permute-start | bytes 1572872 | tf_op jit(solution)/shard_map/ppermute | solution.py:442
  66.9 16.8 %collective-permute-start.14 = (bf16[256,1024]{1,0:T(8,128)(2,1)}, bf16[256,1024]{1,0:T(8,128)(2,1)}, u32[]{:S(2)}, u32[]{:S(2)}) collective-permute-start(bf16[256,1024]{1,0:T(8,128)(2,1)} %collective-permute-done.11.refs_16_), channel_id=1, source_target_pairs={{0,8},{4,20},{8,0},{12,28},{16,24},{20,4},{24,16},{28,12},{1,9},{5... | collective-permute-start | bytes 1572872 | tf_op jit(solution)/shard_map/ppermute | solution.py:436
  67.4 16.8 %collective-permute-start.21 = (bf16[256,1024]{1,0:T(8,128)(2,1)}, bf16[256,1024]{1,0:T(8,128)(2,1)S(1)}, u32[]{:S(2)}, u32[]{:S(2)}) collective-permute-start(bf16[256,1024]{1,0:T(8,128)(2,1)} %collective-permute-done.11.refs_16_), channel_id=1, source_target_pairs={{0,16},{4,12},{8,24},{12,4},{16,0},{20,28},{24,8},{28,20},{1,17},{... | collective-permute-start | bytes 1572872 | tf_op jit(solution)/shard_map/ppermute | solution.py:436
  69.4 20.8 %collective-permute-start.22 = (bf16[256,1024]{1,0:T(8,128)(2,1)}, bf16[256,1024]{1,0:T(8,128)(2,1)}, u32[]{:S(2)}, u32[]{:S(2)}) collective-permute-start(bf16[256,1024]{1,0:T(8,128)(2,1)} %collective-permute-done.3.refs_13_), channel_id=1, source_target_pairs={{0,16},{4,12},{8,24},{12,4},{16,0},{20,28},{24,8},{28,20},{1,17},{... | collective-permute-start | bytes 1572872 | tf_op jit(solution)/shard_map/ppermute | solution.py:436
  70.9 27.4 %collective-permute-start.4 = (bf16[256,1024]{1,0:T(8,128)(2,1)S(1)}, bf16[256,1024]{1,0:T(8,128)(2,1)S(1)}, u32[]{:S(2)}, u32[]{:S(2)}) collective-permute-start(bf16[256,1024]{1,0:T(8,128)(2,1)S(1)} %get-tuple-element.48), channel_id=1, source_target_pairs={{0,2},{1,3},{2,0},{3,1},{4,6},{5,7},{6,4},{7,5},{8,10},{9,11},{10,... | collective-permute-start | bytes 1572872 | tf_op jit(solution)/shard_map/ppermute | solution.py:442
  83.1 15.8 %collective-permute-start.9 = (bf16[256,1024]{1,0:T(8,128)(2,1)}, bf16[256,1024]{1,0:T(8,128)(2,1)}, u32[]{:S(2)}, u32[]{:S(2)}) collective-permute-start(bf16[256,1024]{1,0:T(8,128)(2,1)} %collective-permute-done.5.refs_20_), channel_id=1, source_target_pairs={{0,8},{4,20},{8,0},{12,28},{16,24},{20,4},{24,16},{28,12},{1,9},{5... | collective-permute-start | bytes 1572872 | tf_op jit(solution)/shard_map/ppermute | solution.py:436
  90.2 36.4 %collective-permute-start.23 = (bf16[256,1024]{1,0:T(8,128)(2,1)}, bf16[256,1024]{1,0:T(8,128)(2,1)}, u32[]{:S(2)}, u32[]{:S(2)}) collective-permute-start(bf16[256,1024]{1,0:T(8,128)(2,1)} %collective-permute-done.20.refs_12_), channel_id=1, source_target_pairs={{0,8},{4,20},{8,0},{12,28},{16,24},{20,4},{24,16},{28,12},{1,9},{5... | collective-permute-start | bytes 1572872 | tf_op jit(solution)/shard_map/ppermute | solution.py:436
  91.4 35.7 %collective-permute-start.27 = (bf16[256,1024]{1,0:T(8,128)(2,1)}, bf16[256,1024]{1,0:T(8,128)(2,1)}, u32[]{:S(2)}, u32[]{:S(2)}) collective-permute-start(bf16[256,1024]{1,0:T(8,128)(2,1)} %get-tuple-element.63), channel_id=1, source_target_pairs={{0,3},{1,0},{2,1},{3,2},{4,7},{5,4},{6,5},{7,6},{8,11},{9,8},{10,9... | collective-permute-start | bytes 1572872 | tf_op jit(solution)/shard_map/ppermute | solution.py:442
  93.7 32.9 %collective-permute-start.15 = (bf16[256,1024]{1,0:T(8,128)(2,1)}, bf16[256,1024]{1,0:T(8,128)(2,1)S(1)}, u32[]{:S(2)}, u32[]{:S(2)}) collective-permute-start(bf16[256,1024]{1,0:T(8,128)(2,1)} %collective-permute-done.14.refs_17_), channel_id=1, source_target_pairs={{0,16},{4,12},{8,24},{12,4},{16,0},{20,28},{24,8},{28,20},{1,17},{... | collective-permute-start | bytes 1572872 | tf_op jit(solution)/shard_map/ppermute | solution.py:436
  98.4 20.6 %collective-permute-start.10 = (bf16[256,1024]{1,0:T(8,128)(2,1)}, bf16[256,1024]{1,0:T(8,128)(2,1)S(1)}, u32[]{:S(2)}, u32[]{:S(2)}) collective-permute-start(bf16[256,1024]{1,0:T(8,128)(2,1)} %collective-permute-done.5.refs_20_), channel_id=1, source_target_pairs={{0,16},{4,12},{8,24},{12,4},{16,0},{20,28},{24,8},{28,20},{1,17},{... | collective-permute-start | bytes 1572872 | tf_op jit(solution)/shard_map/ppermute | solution.py:436
  98.9 28.6 %collective-permute-start.28 = (bf16[256,1024]{1,0:T(8,128)(2,1)}, bf16[256,1024]{1,0:T(8,128)(2,1)S(1)}, u32[]{:S(2)}, u32[]{:S(2)}) collective-permute-start(bf16[256,1024]{1,0:T(8,128)(2,1)} %collective-permute-done.20.refs_12_), channel_id=1, source_target_pairs={{0,16},{4,12},{8,24},{12,4},{16,0},{20,28},{24,8},{28,20},{1,17},{... | collective-permute-start | bytes 1572872 | tf_op jit(solution)/shard_map/ppermute | solution.py:436
  119.0 20.6 %collective-permute-start.32 = (bf16[512,1024]{1,0:T(8,128)(2,1)}, bf16[512,1024]{1,0:T(8,128)(2,1)}, u32[]{:S(2)}, u32[]{:S(2)}) collective-permute-start(bf16[512,1024]{1,0:T(8,128)(2,1)} %get-tuple-element.65), channel_id=1, source_target_pairs={{0,4},{4,0},{8,12},{12,8},{16,20},{20,16},{24,28},{28,24},{1,5},{5... | collective-permute-start | bytes 3145736 | tf_op jit(solution)/shard_map/ppermute | solution.py:439
  126.7 18.6 %collective-permute-start.34 = (bf16[512,1024]{1,0:T(8,128)(2,1)}, bf16[512,1024]{1,0:T(8,128)(2,1)}, u32[]{:S(2)}, u32[]{:S(2)}) collective-permute-start(bf16[512,1024]{1,0:T(8,128)(2,1)} %get-tuple-element.67), channel_id=1, source_target_pairs={{0,4},{4,0},{8,12},{12,8},{16,20},{20,16},{24,28},{28,24},{1,5},{5... | collective-permute-start | bytes 3145736 | tf_op jit(solution)/shard_map/ppermute | solution.py:439
  127.1 18.4 %collective-permute-start.35 = (bf16[512,1024]{1,0:T(8,128)(2,1)}, bf16[512,1024]{1,0:T(8,128)(2,1)S(1)}, u32[]{:S(2)}, u32[]{:S(2)}) collective-permute-start(bf16[512,1024]{1,0:T(8,128)(2,1)} %get-tuple-element.68), channel_id=1, source_target_pairs={{0,4},{4,0},{8,12},{12,8},{16,20},{20,16},{24,28},{28,24},{1,5},{5... | collective-permute-start | bytes 3145736 | tf_op jit(solution)/shard_map/ppermute | solution.py:439
  137.9 28.6 %collective-permute-start.16 = (bf16[256,1024]{1,0:T(8,128)(2,1)S(1)}, bf16[256,1024]{1,0:T(8,128)(2,1)S(1)}, u32[]{:S(2)}, u32[]{:S(2)}) collective-permute-start(bf16[256,1024]{1,0:T(8,128)(2,1)S(1)} %collective-permute-done.4.refs_16_), channel_id=1, source_target_pairs={{0,8},{4,20},{8,0},{12,28},{16,24},{20,4},{24,16},{28,12},{1,9},{5... | collective-permute-start | bytes 1572872 | tf_op jit(solution)/shard_map/ppermute | solution.py:436
  139.5 27.0 %collective-permute-start.19 = (bf16[256,1024]{1,0:T(8,128)(2,1)S(1)}, bf16[256,1024]{1,0:T(8,128)(2,1)S(1)}, u32[]{:S(2)}, u32[]{:S(2)}) collective-permute-start(bf16[256,1024]{1,0:T(8,128)(2,1)S(1)} %collective-permute-done.4.refs_16_), channel_id=1, source_target_pairs={{0,16},{4,12},{8,24},{12,4},{16,0},{20,28},{24,8},{28,20},{1,17},{... | collective-permute-start | bytes 1572872 | tf_op jit(solution)/shard_map/ppermute | solution.py:436
  140.0 24.9 %collective-permute-start.18 = (bf16[256,512]{1,0:T(8,128)(2,1)}, bf16[256,512]{1,0:T(8,128)(2,1)S(1)}, u32[]{:S(2)}, u32[]{:S(2)}) collective-permute-start(bf16[256,512]{1,0:T(8,128)(2,1)} %copy-done.31), channel_id=1, source_target_pairs={{0,1},{1,2},{2,3},{3,0},{4,5},{5,6},{6,7},{7,4},{8,9},{9,10},{10,1... | collective-permute-start | bytes 786440 | tf_op jit(solution)/shard_map/ppermute | solution.py:442
  145.3 23.4 %collective-permute-start.24 = (bf16[256,1024]{1,0:T(8,128)(2,1)}, bf16[256,1024]{1,0:T(8,128)(2,1)S(1)}, u32[]{:S(2)}, u32[]{:S(2)}) collective-permute-start(bf16[256,1024]{1,0:T(8,128)(2,1)} %collective-permute-done.23.refs_13_), channel_id=1, source_target_pairs={{0,16},{4,12},{8,24},{12,4},{16,0},{20,28},{24,8},{28,20},{1,17},{... | collective-permute-start | bytes 1572872 | tf_op jit(solution)/shard_map/ppermute | solution.py:436
  145.5 21.5 %collective-permute-start.30 = (bf16[256,1024]{1,0:T(8,128)(2,1)}, bf16[256,1024]{1,0:T(8,128)(2,1)S(1)}, u32[]{:S(2)}, u32[]{:S(2)}) collective-permute-start(bf16[256,1024]{1,0:T(8,128)(2,1)} %collective-permute-done.27.refs_20_), channel_id=1, source_target_pairs={{0,8},{4,20},{8,0},{12,28},{16,24},{20,4},{24,16},{28,12},{1,9},{5... | collective-permute-start | bytes 1572872 | tf_op jit(solution)/shard_map/ppermute | solution.py:436
  166.5 41.4 %collective-permute-start.36 = (f32[512,1024]{1,0:T(8,128)}, f32[512,1024]{1,0:T(8,128)S(1)}, u32[]{:S(2)}, u32[]{:S(2)}) collective-permute-start(f32[512,1024]{1,0:T(8,128)} %get-tuple-element.73), channel_id=1, source_target_pairs={{0,4},{4,0},{8,12},{12,8},{16,20},{20,16},{24,28},{28,24},{1,5},{5... | collective-permute-start | bytes 6291464 | tf_op jit(solution)/shard_map/ppermute | solution.py:439
  166.5 16.3 %collective-permute-start.43 = (bf16[256,1024]{1,0:T(8,128)(2,1)S(1)}, bf16[256,1024]{1,0:T(8,128)(2,1)S(1)}, u32[]{:S(2)}, u32[]{:S(2)}) collective-permute-start(bf16[256,1024]{1,0:T(8,128)(2,1)S(1)} %collective-permute-done.16.refs_17_), channel_id=1, source_target_pairs={{0,16},{4,12},{8,24},{12,4},{16,0},{20,28},{24,8},{28,20},{1,17},{... | collective-permute-start | bytes 1572872 | tf_op jit(solution)/shard_map/ppermute | solution.py:436
  167.1 21.3 %collective-permute-start.31 = (bf16[256,1024]{1,0:T(8,128)(2,1)S(1)}, bf16[256,1024]{1,0:T(8,128)(2,1)S(1)}, u32[]{:S(2)}, u32[]{:S(2)}) collective-permute-start(bf16[256,1024]{1,0:T(8,128)(2,1)S(1)} %collective-permute-done.30.refs_21_), channel_id=1, source_target_pairs={{0,16},{4,12},{8,24},{12,4},{16,0},{20,28},{24,8},{28,20},{1,17},{... | collective-permute-start | bytes 1572872 | tf_op jit(solution)/shard_map/ppermute | solution.py:436
  168.7 35.5 %collective-permute-start.41 = (bf16[256,512]{1,0:T(8,128)(2,1)S(1)}, bf16[256,512]{1,0:T(8,128)(2,1)S(1)}, u32[]{:S(2)}, u32[]{:S(2)}) collective-permute-start(bf16[256,512]{1,0:T(8,128)(2,1)S(1)} %copy-done.30), channel_id=1, source_target_pairs={{0,2},{1,3},{2,0},{3,1},{4,6},{5,7},{6,4},{7,5},{8,10},{9,11},{10,... | collective-permute-start | bytes 786440 | tf_op jit(solution)/shard_map/ppermute | solution.py:442
  174.4 32.5 %collective-permute-start.25 = (bf16[256,512]{1,0:T(8,128)(2,1)S(1)}, bf16[256,512]{1,0:T(8,128)(2,1)S(1)}, u32[]{:S(2)}, u32[]{:S(2)}) collective-permute-start(bf16[256,512]{1,0:T(8,128)(2,1)S(1)} %collective-permute-done.18.refs_10_), channel_id=1, source_target_pairs={{0,8},{4,20},{8,0},{12,28},{16,24},{20,4},{24,16},{28,12},{1,9},{5... | collective-permute-start | bytes 786440 | tf_op jit(solution)/shard_map/ppermute | solution.py:436
  202.5 37.7 %collective-permute-start.53 = (f32[512,1024]{1,0:T(8,128)}, f32[512,1024]{1,0:T(8,128)}, u32[]{:S(2)}, u32[]{:S(2)}) collective-permute-start(f32[512,1024]{1,0:T(8,128)} %get-tuple-element.83), channel_id=1, source_target_pairs={{0,4},{4,0},{8,12},{12,8},{16,20},{20,16},{24,28},{28,24},{1,5},{5... | collective-permute-start | bytes 6291464 | tf_op jit(solution)/shard_map/ppermute | solution.py:439
  (70 other events, 793.6 us)
